TPU v7x, 256 devices: a whole 4x4x8 slice. The times are simulated.
256 devices in a mesh: dp: 16 (over y_hi, z), ctx: 16 (over y_lo, x, core).
Axes of the slice: x: 4, y: 4 (y_hi: 2, y_lo: 2; y = y_hi * 2 + y_lo), z: 8, core: 2. Of those that a mesh axis runs over, the one named last changes fastest.
Arguments:
- queries: bfloat16 [49152, 4096], P(('dp', 'ctx')), may hold values from -140 to 140
- keys: bfloat16 [49152, 512], P(('dp', 'ctx')), may hold values from -5 to 5
- values: bfloat16 [49152, 512], P(('dp', 'ctx')), may hold values from -6 to 6
- block_order: int32 [16, 16], P('dp'), may hold values from 0 to 15, each once within a row
- query_maps: float32 [32, 128, 64], P('ctx'), may hold values from -0.5 to 0.5
- key_maps: float32 [32, 128, 64], P('ctx'), may hold values from -0.5 to 0.5
Outputs:
- teacher_out: bfloat16 [49152, 4096], P(('dp', 'ctx'))
- query_grads: float32 [32, 128, 64], P('ctx')
- key_grads: float32 [32, 128, 64], P('ctx')
Inputs may be any that keep to these rules, and one draw needn't show every extreme that they name: Each row of block_order names every block once.
All inputs are finite; a program needn't handle non-finite values.
Results may differ from a plain program's by a relative error of at most 0.005.
Values may be sent and summed in bfloat16 or wider, within the bound.
No kernel may reach another device: no remote copies, remote signals or barrier semaphores. Data moves between devices by JAX's collectives and lax.ppermute only.
A program may use at most 128 MiB of HBM per device.

v0:
```python
import jax
import jax.numpy as jnp
import numpy as np
from jax import lax
from jax.sharding import PartitionSpec as P

SPAN = 256


HIGHEST = lax.Precision.HIGHEST


def features(inputs, weights):
    logits = jnp.dot(inputs.astype(jnp.float32), weights, precision=HIGHEST)
    return jnp.concatenate(
        [jax.nn.softmax(logits, axis=-1), jax.nn.softmax(-logits, axis=-1)], axis=-1
    )


def student_loss(query_map, key_map, query_head, key_head, value_head, target_head, loss_scale):
    query_feats = features(query_head, query_map)
    key_feats = features(key_head, key_map)
    length = query_head.shape[0]
    span_count = length // SPAN
    feat_width = query_feats.shape[1]
    head_dim = value_head.shape[1]
    query_blocks = query_feats.reshape(span_count, SPAN, feat_width)
    key_blocks = key_feats.reshape(span_count, SPAN, feat_width)
    value_blocks = value_head.astype(jnp.float32).reshape(span_count, SPAN, head_dim)
    lower_mask = jnp.tril(jnp.ones((SPAN, SPAN), jnp.float32))

    def advance(state_pair, block_data):
        state, normal_sum = state_pair
        query_rows, key_rows, value_rows = block_data
        within = jnp.dot(query_rows, key_rows.T, precision=HIGHEST) * lower_mask
        numerator = jnp.dot(within, value_rows, precision=HIGHEST) + jnp.dot(
            query_rows, state, precision=HIGHEST
        )
        denominator = jnp.sum(within, axis=1) + jnp.dot(query_rows, normal_sum, precision=HIGHEST)
        updated = (
            state + jnp.dot(key_rows.T, value_rows, precision=HIGHEST),
            normal_sum + jnp.sum(key_rows, axis=0),
        )
        return (updated, numerator / denominator[:, None])

    initial = (
        jnp.zeros((feat_width, head_dim), jnp.float32),
        jnp.zeros((feat_width,), jnp.float32),
    )
    unused_state, outputs = lax.scan(advance, initial, (query_blocks, key_blocks, value_blocks))
    mismatch = outputs.reshape(length, head_dim) - target_head.astype(jnp.float32)
    return jnp.sum(mismatch * mismatch) * loss_scale


def on_device(queries, keys, values, block_order, query_maps, key_maps):
    local_rows = queries.shape[0]
    ctx_count = lax.axis_size("ctx")
    heads_dev = query_maps.shape[0]
    head_dim = query_maps.shape[1]
    all_heads = heads_dev * ctx_count
    kv_heads = keys.shape[1] // head_dim
    group_size = all_heads // kv_heads
    kv_dev = max(1, heads_dev // group_size)
    seq_len = local_rows * ctx_count
    score_scale = head_dim ** (-0.5)
    block_table = block_order[0]
    ctx_index = lax.axis_index("ctx")
    block_ids = jnp.arange(ctx_count, dtype=jnp.int32)
    inverse = jnp.sum(
        jnp.where(block_table[:, None] == block_ids[None, :], block_ids[:, None], 0), axis=0
    )
    picked = (
        np.arange(ctx_count)[:, None] * heads_dev // group_size + np.arange(kv_dev)[None, :]
    ).reshape(-1)
    kv_local = np.arange(heads_dev) // group_size
    query_pack = queries.reshape(local_rows, ctx_count, heads_dev * head_dim)
    key_pack = keys.reshape(local_rows, kv_heads, head_dim)[:, picked].reshape(
        local_rows, ctx_count, kv_dev * head_dim
    )
    value_pack = values.reshape(local_rows, kv_heads, head_dim)[:, picked].reshape(
        local_rows, ctx_count, kv_dev * head_dim
    )

    def to_sequence(stored):
        shape_in = stored.shape
        blocked = stored.reshape((ctx_count, local_rows) + shape_in[1:])
        return jnp.take(blocked, inverse, axis=0).reshape(shape_in)

    own_pos = block_table[ctx_index] * local_rows + jnp.arange(local_rows, dtype=jnp.int32)
    query_heads = queries.reshape(local_rows, kv_heads, group_size, head_dim).transpose(1, 2, 0, 3)
    initial = (
        jnp.full((kv_heads, group_size, local_rows), -1e30, jnp.float32),
        jnp.zeros((kv_heads, group_size, local_rows), jnp.float32),
        jnp.zeros((kv_heads, group_size, local_rows, head_dim), jnp.float32),
    )
    key_piece = lax.all_gather(keys, "ctx", axis=0, tiled=True)
    value_piece = lax.all_gather(values, "ctx", axis=0, tiled=True)
    piece_rows = key_piece.shape[0]
    key_rows = jnp.arange(piece_rows, dtype=jnp.int32)
    key_blocks = key_rows // local_rows
    key_pos = (
        jnp.sum(
            jnp.where(key_blocks[:, None] == block_ids[None, :], block_table[None, :], 0), axis=1
        )
        * local_rows
        + key_rows % local_rows
    )
    causal_mask = key_pos[None, :] <= own_pos[:, None]
    key_heads = key_piece.reshape(piece_rows, kv_heads, head_dim).transpose(1, 0, 2)
    value_heads = value_piece.reshape(piece_rows, kv_heads, head_dim).transpose(1, 0, 2)

    def per_group(operands):
        query_group, key_group, value_group, run_max, run_total, run_sum = operands
        scores = (
            jnp.einsum("gqd,nd->gqn", query_group, key_group, preferred_element_type=jnp.float32)
            * score_scale
        )
        scores = jnp.where(causal_mask[None], scores, -1e30)
        new_max = jnp.maximum(run_max, jnp.max(scores, axis=-1))
        weights = jnp.where(causal_mask[None], jnp.exp(scores - new_max[..., None]), 0.0)
        rescale = jnp.exp(run_max - new_max)
        new_total = run_total * rescale + jnp.sum(weights, axis=-1)
        new_sum = run_sum * rescale[..., None] + jnp.einsum(
            "gqn,nd->gqd",
            weights.astype(jnp.bfloat16),
            value_group,
            preferred_element_type=jnp.float32,
        )
        return (new_max, new_total, new_sum)

    run_max, run_total, run_sum = lax.map(
        per_group, (query_heads, key_heads, value_heads) + tuple(initial)
    )
    teacher_out = (
        (run_sum / run_total[..., None])
        .astype(jnp.bfloat16)
        .transpose(2, 0, 1, 3)
        .reshape(local_rows, all_heads * head_dim)
    )
    gathered = (
        lax.all_to_all(query_pack, "ctx", split_axis=1, concat_axis=0, tiled=True),
        lax.all_to_all(key_pack, "ctx", split_axis=1, concat_axis=0, tiled=True),
        lax.all_to_all(value_pack, "ctx", split_axis=1, concat_axis=0, tiled=True),
        lax.all_to_all(
            teacher_out.reshape(local_rows, ctx_count, heads_dev * head_dim),
            "ctx",
            split_axis=1,
            concat_axis=0,
            tiled=True,
        ),
    )
    seq_queries, seq_keys, seq_values, seq_teacher = [
        to_sequence(member.reshape(seq_len, member.shape[2])) for member in gathered
    ]
    query_heads = seq_queries.reshape(seq_len, heads_dev, head_dim).transpose(1, 0, 2)
    key_heads = seq_keys.reshape(seq_len, kv_dev, head_dim)[:, kv_local].transpose(1, 0, 2)
    value_heads = seq_values.reshape(seq_len, kv_dev, head_dim)[:, kv_local].transpose(1, 0, 2)
    target_heads = seq_teacher.reshape(seq_len, heads_dev, head_dim).transpose(1, 0, 2)
    loss_scale = 1.0 / lax.axis_size("dp")

    def head_grads(operands):
        query_map, key_map, query_head, key_head, value_head, target_head = operands
        return jax.grad(student_loss, argnums=(0, 1))(
            query_map, key_map, query_head, key_head, value_head, target_head, loss_scale
        )

    grads_query, grads_key = lax.map(
        head_grads, (query_maps, key_maps, query_heads, key_heads, value_heads, target_heads)
    )
    grads_query, grads_key = lax.psum((grads_query, grads_key), "dp")
    return (teacher_out, grads_query, grads_key)


def solution(mesh):
    in_specs = (
        P(("dp", "ctx"), None),
        P(("dp", "ctx"), None),
        P(("dp", "ctx"), None),
        P("dp", None),
        P("ctx", None, None),
        P("ctx", None, None),
    )
    out_specs = (P(("dp", "ctx"), None), P("ctx", None, None), P("ctx", None, None))
    return jax.shard_map(
        on_device, mesh=mesh, in_specs=in_specs, out_specs=out_specs, check_vma=False
    )
```

profile of v0, /device:TPU:2, one launch (start us, length us, event | category | flops | bytes accessed | tf_op | source)
XLA Modules:
  0.0 1008.1 jit_solution(1495857224932926438)
XLA Ops:
  11.8 5.9 all-to-all-start.2
  19.3 10.5 %all-to-all-done.2 = bf16[192,16,128]{2,0,1:T(8,128)(2,1)S(1)} async-done(((bf16[192,16,128]{2,0,1:T(8,128)(2,1)}), bf16[192,16,128]{2,0,1:T(8,128)(2,1)S(1)}, u32[]{:S(2)}, u32[]{:S(2)}) %all-to-all-start.2) | async-done | bytes 786464 | tf_op jit(solution)/shard_map/all_to_all | solution.py:143
  29.8 6.4 all-to-all-start.1
  42.1 16.2 %all-gather.3.cloned.1.call-done = bf16[3072,512]{1,0:T(8,128)(2,1)} async-done(((bf16[192,512]{1,0:T(8,128)(2,1)}), bf16[3072,512]{1,0:T(8,128)(2,1)}) %all-gather.3.cloned.1.call-update) | async-done | bytes 3145744 | tf_op jit(solution)/shard_map/all_gather | solution.py:96
  58.3 4.7 copy.87
  63.0 37.6 %all-gather.5.cloned.1.call-done = bf16[3072,512]{1,0:T(8,128)(2,1)} async-done(((bf16[192,512]{1,0:T(8,128)(2,1)}), bf16[3072,512]{1,0:T(8,128)(2,1)}) %all-gather.5.cloned.1.call-update) | async-done | bytes 3145744 | tf_op jit(solution)/shard_map/all_gather | solution.py:97
  100.6 4.8 copy.88
  106.3 4.8 all-to-all-start
  111.1 127.4 %while.122 = (s32[]{:T(128)}, f32[4,8,192]{2,1,0:T(8,128)S(1)}, f32[4,8,192,128]{3,2,1,0:T(8,128)}, bf16[4,8,192,128]{3,1,0,2:T(8,128)(2,1)S(1)}, bf16[4,3072,12...) while((s32[]{:T(128)}, f32[4,8,192]{2,1,0:T(8,128)S(1)}, ...), condition=%wide.region_4.5_spmd.clone, body=%wide.region_1.4_spmd.clone.sunk | while | flops 2478054912 | bytes 62609264 | solution.py:131
  111.6 9.6 fusion.238
  121.2 11.8 %fusion.239 = f32[8,192]{1,0:T(8,128)S(1)} fusion(f32[8,192,3072]{2,1,0:T(8,128)} %get-tuple-element.1459, f32[8,192]{1,0:T(8,128)S(1)} %get-tuple-element.1461, pred[192,3072]{1,0:T(8,128)(4,1)S(1)} %broadcast_compare_fusion.2), kind=kLoop, calls=%fused_computation.13.clone.1 | loop fusion | flops 23591424 | bytes 19476480 | tf_op jit(solution)/shard_map/while/body/eval_jaxpr/reduce_sum | solution.py:122
  133.0 10.1 fusion.240
  143.5 9.6 fusion.238
  153.1 11.8 %fusion.239 = f32[8,192]{1,0:T(8,128)S(1)} fusion(f32[8,192,3072]{2,1,0:T(8,128)} %get-tuple-element.1459, f32[8,192]{1,0:T(8,128)S(1)} %get-tuple-element.1461, pred[192,3072]{1,0:T(8,128)(4,1)S(1)} %broadcast_compare_fusion.2), kind=kLoop, calls=%fused_computation.13.clone.1 | loop fusion | flops 23591424 | bytes 19476480 | tf_op jit(solution)/shard_map/while/body/eval_jaxpr/reduce_sum | solution.py:122
  164.9 10.0 fusion.240
  175.3 9.6 fusion.238
  184.9 11.8 %fusion.239 = f32[8,192]{1,0:T(8,128)S(1)} fusion(f32[8,192,3072]{2,1,0:T(8,128)} %get-tuple-element.1459, f32[8,192]{1,0:T(8,128)S(1)} %get-tuple-element.1461, pred[192,3072]{1,0:T(8,128)(4,1)S(1)} %broadcast_compare_fusion.2), kind=kLoop, calls=%fused_computation.13.clone.1 | loop fusion | flops 23591424 | bytes 19476480 | tf_op jit(solution)/shard_map/while/body/eval_jaxpr/reduce_sum | solution.py:122
  196.6 10.0 fusion.240
  207.0 9.6 fusion.238
  216.7 11.8 %fusion.239 = f32[8,192]{1,0:T(8,128)S(1)} fusion(f32[8,192,3072]{2,1,0:T(8,128)} %get-tuple-element.1459, f32[8,192]{1,0:T(8,128)S(1)} %get-tuple-element.1461, pred[192,3072]{1,0:T(8,128)(4,1)S(1)} %broadcast_compare_fusion.2), kind=kLoop, calls=%fused_computation.13.clone.1 | loop fusion | flops 23591424 | bytes 19476480 | tf_op jit(solution)/shard_map/while/body/eval_jaxpr/reduce_sum | solution.py:122
  228.4 10.1 fusion.240
  245.0 5.9 all-to-all-start.3
  259.9 12.4 %all-to-all-done.3 = bf16[192,16,256]{2,0,1:T(8,128)(2,1)S(1)} async-done(((bf16[192,16,256]{2,0,1:T(8,128)(2,1)}), bf16[192,16,256]{2,0,1:T(8,128)(2,1)S(1)}, u32[]{:S(2)}, u32[]{:S(2)}) %all-to-all-start.3) | async-done | bytes 1572896 | tf_op jit(solution)/shard_map/all_to_all | solution.py:144
  274.1 3.4 broadcast_select_fusion.3
  285.7 558.5 %while.121 = (s32[]{:T(128)}, f32[2,128,64]{1,2,0:T(8,128)}, f32[2,128,64]{1,2,0:T(8,128)}, bf16[2,3072,128]{2,1,0:T(8,128)(2,1)}, f32[2,128,64]{1,2,0:T(8,128)}...) while((s32[]{:T(128)}, f32[2,128,64]{1,2,0:T(8,128)}, ...), condition=%wide.region_26.29_spmd, body=%wide.region_6.28_spmd.sunk | while | flops 1980548096 | bytes 111246568 | solution.py:167
  299.2 117.3 %while.123 = (s32[]{:T(128)}, f32[128,128]{1,0:T(8,128)S(1)}, f32[128]{0:T(128)}, f32[12,256,128]{2,1,0:T(8,128)}, f32[12,128,256]{2,1,0:T(8,128)}, /*index=5*/f...) while((s32[]{:T(128)}, f32[128,128]{1,0:T(8,128)S(1)}, ...), condition=%wide.region_18.20_spmd.clone, body=%wide.region_15.19_spmd.clone.sunk | while | flops 302809856 | bytes 3096775 | solution.py:50
  416.6 3.6 fusion.231
  421.6 125.4 %while.124 = (s32[]{:T(128)}, f32[128,128]{1,0:T(8,128)S(1)}, f32[128]{0:T(128)S(1)}, f32[12,256,128]{2,1,0:T(8,128)S(1)}, f32[12,256,128]{2,1,0:T(8,128)}, /*in...) while((s32[]{:T(128)}, f32[128,128]{1,0:T(8,128)S(1)}, ...), condition=%wide.region_21.23_spmd.clone, body=%wide.region_19.22_spmd.clone.sunk | while | flops 454050048 | bytes 3301072 | solution.py:50
  578.5 117.3 %while.123 = (s32[]{:T(128)}, f32[128,128]{1,0:T(8,128)S(1)}, f32[128]{0:T(128)}, f32[12,256,128]{2,1,0:T(8,128)}, f32[12,128,256]{2,1,0:T(8,128)}, /*index=5*/f...) while((s32[]{:T(128)}, f32[128,128]{1,0:T(8,128)S(1)}, ...), condition=%wide.region_18.20_spmd.clone, body=%wide.region_15.19_spmd.clone.sunk | while | flops 302809856 | bytes 3096775 | solution.py:50
  695.8 3.6 fusion.231
  700.8 125.4 %while.124 = (s32[]{:T(128)}, f32[128,128]{1,0:T(8,128)S(1)}, f32[128]{0:T(128)S(1)}, f32[12,256,128]{2,1,0:T(8,128)S(1)}, f32[12,256,128]{2,1,0:T(8,128)}, /*in...) while((s32[]{:T(128)}, f32[128,128]{1,0:T(8,128)S(1)}, ...), condition=%wide.region_21.23_spmd.clone, body=%wide.region_19.22_spmd.clone.sunk | while | flops 454050048 | bytes 3301072 | solution.py:50
  847.4 151.2 %all-reduce.3.cloned.1.call-done = (f32[2,128,64]{1,2,0:T(8,128)}, f32[2,128,64]{1,2,0:T(8,128)}) async-done(((f32[2,128,64]{1,2,0:T(8,128)}, f32[2,128,64]{1,2,0:T(8,128)}), (f32[2,128,64]{1,2,0:T(8,128)}, f32[2,128,64]{1,2,0:T(8,128)})) %all-reduce.3.cloned.1.call-update) | async-done | bytes 131088 | tf_op jit(solution)/shard_map/psum | solution.py:170
  (880 shorter events, 594.8 us)
Async XLA Ops:
  7.2 51.1 %all-gather.3.cloned.1.call-start = ((), (), s32[]{:S(2)}) async-start(), calls=%async_computation.4 | async-start | bytes 3342336 | tf_op jit(solution)/shard_map/all_gather | solution.py:96
  7.9 92.7 %all-gather.5.cloned.1.call-start = ((), (), s32[]{:S(2)}) async-start(), calls=%async_computation.5 | async-start | bytes 3342336 | tf_op jit(solution)/shard_map/all_gather | solution.py:97
  10.3 7.4 copy-start.32
  11.8 18.0 %all-to-all-start.2 = ((bf16[192,16,128]{2,0,1:T(8,128)(2,1)}), bf16[192,16,128]{2,0,1:T(8,128)(2,1)S(1)}, u32[]{:S(2)}, u32[]{:S(2)}) async-start(bf16[192,16,128]{2,0,1:T(8,128)(2,1)} %bitcast.29), calls=%async_computation.2 | async-start | bytes 1572864 | tf_op jit(solution)/shard_map/all_to_all | solution.py:143
  29.8 6.5 copy-start.17
  29.8 75.6 %all-to-all-start.1 = ((bf16[192,16,128]{2,0,1:T(8,128)(2,1)}), bf16[192,16,128]{2,0,1:T(8,128)(2,1)S(1)}, u32[]{:S(2)}, u32[]{:S(2)}) async-start(bf16[192,16,128]{2,0,1:T(8,128)(2,1)} %bitcast.24), calls=%async_computation.1 | async-start | bytes 1572864 | tf_op jit(solution)/shard_map/all_to_all | solution.py:142
  38.0 2.8 copy-start.37
  106.3 138.7 %all-to-all-start = ((bf16[192,16,256]{2,0,1:T(8,128)(2,1)}), bf16[192,16,256]{2,0,1:T(8,128)(2,1)}, u32[]{:S(2)}, u32[]{:S(2)}) async-start(bf16[192,16,256]{2,0,1:T(8,128)(2,1)} %bitcast.348), calls=%async_computation | async-start | bytes 3145728 | tf_op jit(solution)/shard_map/all_to_all | solution.py:141
  245.0 6.1 copy-start.18
  245.0 27.3 %all-to-all-start.3 = ((bf16[192,16,256]{2,0,1:T(8,128)(2,1)}), bf16[192,16,256]{2,0,1:T(8,128)(2,1)S(1)}, u32[]{:S(2)}, u32[]{:S(2)}) async-start(bf16[192,16,256]{2,0,1:T(8,128)(2,1)} %copy.97), calls=%async_computation.3 | async-start | bytes 3145728 | tf_op jit(solution)/shard_map/all_to_all | solution.py:144
  250.9 1.8 copy-start.20
  250.9 747.7 %all-reduce.3.cloned.1.call-start = ((), (), s32[]{:S(2)}) async-start(), calls=%async_computation.6 | async-start | bytes 262144 | tf_op jit(solution)/shard_map/psum | solution.py:170
  252.7 1.5 copy-start.21
  416.6 3.6 copy-start.5
  549.2 2.0 copy-start.6
  551.2 1.5 copy-start.4
  552.7 1.7 copy-start.8
  552.7 1.7 copy-start.33
  554.4 2.2 copy-start
  556.5 1.7 copy-start.34
  561.5 1.8 copy-start.7
  561.5 1.9 copy-start.9
  561.5 1.9 copy-start.35
  695.8 3.6 copy-start.5
  828.5 2.0 copy-start.6
  831.9 1.7 copy-start.8
  831.9 1.7 copy-start.33
  833.6 2.2 copy-start
  835.8 1.7 copy-start.34
  840.7 1.8 copy-start.7
  840.7 1.9 copy-start.9
  840.7 1.9 copy-start.35
  (43 other events, 47.5 us)
Sparse Core Ops, SparseCore 0:
  9.8 48.4 all-gather.2
  60.2 40.4 all-gather.4
  844.3 154.3 all-reduce.2
where the time goes:
time: 1020 us; the launch traced here: 1010 us
  matrix products  356 us (35%)
  waiting for transfers between devices  229 us (22%)
  local copies, waits for them, and re-layouts  198 us (19%)
  other arithmetic  184 us (18%)
  starting transfers between devices  23.2 us (2%)
  between operations  13.9 us (1%)
    psum x1, waiting for transfers between devices, on_device(): grads_query, grads_key = lax.psum((grads_query, grads_key), 'dp')  151 us
    dynamic_update_slice x72, local copies, waits for them, and re-layouts, student_loss(): lax.scan(advance, initial, (query_blocks, key_blocks, value_blocks))  76.2 us
    dot_general x72, matrix products, advance(): within = jnp.dot(query_rows, key_rows.T, precision=HIGHEST) * lower_mask  70.4 us
    dot_general x72, matrix products, advance(): jnp.dot(query_rows, state, precision=HIGHEST)  68 us
    dot_general x48, matrix products, advance(): jnp.dot(within, value_rows, precision=HIGHEST)  64.9 us
    reduce_sum x4, other arithmetic, per_group(): new_total = run_total * rescale + jnp.sum(weights, axis=-1)  47 us
    dot_general x4, matrix products, per_group(): jnp.einsum('gqn,nd->gqd', weights.astype(jnp.bfloat16), value_group, pref...  40.1 us
    dot_general x4, matrix products, per_group(): jnp.einsum('gqd,nd->gqn', query_group, key_group, preferred_element_type=...  38.4 us
  transfers between devices with their start and end apart: 7, of which 5 were waited for; matrix products, arithmetic and copies ran while one was open for 16% of the time, Pallas kernels for 0%

commit v1 on v0

v1 whole, which is shorter than its diff:
```python
import functools
import math

import jax
import jax.numpy as jnp
import numpy as np
from jax import lax
from jax.experimental import pallas as pl
from jax.experimental.pallas import tpu as pltpu
from jax.sharding import PartitionSpec as P

BF = jnp.bfloat16
F32 = jnp.float32
CHUNK = 256


def mm(a, b, ca=1, cb=0):
    return lax.dot_general(a, b, (((ca,), (cb,)), ((), ())), preferred_element_type=F32)


def split(x):
    high = x.astype(BF)
    return high, (x - high.astype(F32)).astype(BF)


def lower_mask():
    rows = lax.broadcasted_iota(jnp.int32, (CHUNK, CHUNK), 0)
    cols = lax.broadcasted_iota(jnp.int32, (CHUNK, CHUNK), 1)
    return cols <= rows


def teacher_kernel(scale, place, q_ref, k_ref, v_ref, o_ref, qs, ks, vs, os, scores, probs):
    blocks, rows, width = k_ref.shape
    tiles = blocks * rows // CHUNK
    for p in range(blocks):
        b = place[p]
        span = pl.ds(p * rows, rows)
        qs[span, :] = q_ref[b]
        ks[span, :] = k_ref[b]
        vs[span, :width] = v_ref[b]
    vs[:, width:] = jnp.ones((blocks * rows, width), BF)
    mask = lower_mask()
    tops = {}

    def first(i, j):
        s = mm(qs[pl.ds(i * CHUNK, CHUNK), :], ks[pl.ds(j * CHUNK, CHUNK), :], 1, 1)
        if i == j:
            s = jnp.where(mask, s, -1e30)
        scores[i % 2, j] = s
        top = functools.reduce(
            jnp.maximum, [s[:, g * width : (g + 1) * width] for g in range(CHUNK // width)]
        )
        tops[i] = top if j == 0 else jnp.maximum(tops[i], top)

    def second(i, j, peak):
        p = jnp.exp2((scores[i % 2, j] - peak) * scale)
        probs[i % 2, :, j * CHUNK : (j + 1) * CHUNK] = p.astype(BF)

    def finish(i):
        keys = (i + 1) * CHUNK
        both = mm(probs[i % 2, :, :keys], vs[:keys, :])
        os[pl.ds(i * CHUNK, CHUNK), :] = (both[:, :width] / both[:, width:]).astype(BF)

    for i in range(tiles + 1):
        if i > 0:
            peak = jnp.max(tops[i - 1], axis=1, keepdims=True)
        for j in range(i + 1):
            if i < tiles:
                first(i, j)
            if i > 0 and j < i:
                second(i - 1, j, peak)
        if i > 0:
            finish(i - 1)
    for p in range(blocks):
        o_ref[place[p]] = os[pl.ds(p * rows, rows), :]


def teacher(place, q, k, v):
    blocks, rows, width = k.shape
    n = blocks * rows
    tiles = n // CHUNK
    whole = pl.BlockSpec(memory_space=pltpu.VMEM)
    return pl.pallas_call(
        functools.partial(teacher_kernel, math.log2(math.e) * width**-0.5),
        out_shape=jax.ShapeDtypeStruct((blocks, rows, width), BF),
        in_specs=[pl.BlockSpec(memory_space=pltpu.SMEM), whole, whole, whole],
        out_specs=whole,
        scratch_shapes=[
            pltpu.VMEM((n, width), BF),
            pltpu.VMEM((n, width), BF),
            pltpu.VMEM((n, 2 * width), BF),
            pltpu.VMEM((n, width), BF),
            pltpu.VMEM((2, tiles, CHUNK, CHUNK), F32),
            pltpu.VMEM((2, CHUNK, n), BF),
        ],
        compiler_params=pltpu.CompilerParams(vmem_limit_bytes=48 * 2**20),
        cost_estimate=pl.CostEstimate(
            flops=2 * n * n * width, bytes_accessed=8 * n * width, transcendentals=n * n // 2
        ),
        name="teacher",
    )(place, q, k, v)


def twice(x, axis):
    return jnp.concatenate([x, x], axis=axis)


def student_kernel(
    loss_scale, place, q0, q1, k_ref, v_ref, t0, t1, wq, wk, o_ref, qs, ks, vs, ts, pqs, pks, zqs, zks, das, dds
):
    blocks, rows, width = k_ref.shape
    n = blocks * rows
    tiles = n // CHUNK
    heads = 2
    half = width // 2
    for p in range(blocks):
        b = place[p]
        span = pl.ds(p * rows, rows)
        qs[0, span, :] = q0[b]
        qs[1, span, :] = q1[b]
        ts[0, span, :] = t0[b]
        ts[1, span, :] = t1[b]
        ks[span, :] = k_ref[b]
        vs[span, :width] = v_ref[b]
    vs[:, width:] = jnp.ones((n, width), BF)
    mask = lower_mask()
    lanes = lax.broadcasted_iota(jnp.int32, (CHUNK, width), 1)
    left = lanes < half
    same = (lax.broadcasted_iota(jnp.int32, (2 * width, width), 0) // half % 2) == (
        lax.broadcasted_iota(jnp.int32, (2 * width, width), 1) // half
    )
    group = jnp.where(same, 1.0, 0.0).astype(BF)

    def halves_sum(x):
        return mm(jnp.concatenate(split(x), axis=1), group)

    def wide(w):
        return jnp.concatenate(split(jnp.concatenate([w, -w], axis=1)), axis=1)

    def features(x, w):
        both = mm(x, w)
        z = both[:, :width] + both[:, width:]
        top = jnp.max(jnp.where(left, z, -jnp.inf), axis=1, keepdims=True)
        other = jnp.max(jnp.where(left, -jnp.inf, z), axis=1, keepdims=True)
        e = jnp.exp(z - jnp.where(left, top, other))
        return jnp.concatenate(split(e / halves_sum(e)), axis=1)

    def back(feats, d):
        p = feats[:, :width].astype(F32) + feats[:, width:].astype(F32)
        x = p * d
        return jnp.concatenate(split(x - p * halves_sum(x)), axis=1)

    wqs = [wide(wq[h]) for h in range(heads)]
    wks = [wide(wk[h]) for h in range(heads)]
    states = [jnp.zeros((width, 2 * width), F32) for _ in range(heads)]
    for c in range(tiles):
        at = slice(c * CHUNK, (c + 1) * CHUNK)
        v1 = vs[at, :]
        for h in range(heads):
            pq = features(qs[h, at, :], wqs[h])
            pk = features(ks[at, :], wks[h])
            pqs[h, at, :] = pq
            pks[h, at, :] = pk
            pk_high = pk[:, :width]
            within = jnp.where(mask, mm(pq, twice(pk_high, 1), 1, 1), 0.0).astype(BF)
            state = states[h].astype(BF)
            both = mm(
                jnp.concatenate([within, pq], axis=1), jnp.concatenate([v1, state, state], axis=0)
            )
            inverse = 1.0 / both[:, width:]
            out = both[:, :width] * inverse
            g = (out - ts[h, at, :].astype(F32)) * (2.0 * loss_scale)
            dd = -jnp.sum(g * out, axis=1, keepdims=True) * inverse
            dd_high, dd_low = split(dd)
            dd_pair = jnp.where(
                lanes == 0, dd_high.astype(F32), jnp.where(lanes == 1, dd_low.astype(F32), 0.0)
            ).astype(BF)
            d = jnp.concatenate([(g * inverse).astype(BF), dd_pair], axis=1)
            da = jnp.where(mask, mm(d, v1, 1, 1), 0.0).astype(BF)
            das[h, c] = da
            dds[h, at, :] = d
            dp = mm(da, pk)
            dp = dp[:, :width] + dp[:, width:] + mm(d, state, 1, 1)
            zqs[h, at, :] = back(pq, dp)
            states[h] = states[h] + mm(pk_high, v1, 0, 0)
    sums = [jnp.zeros((width, 2 * width), F32) for _ in range(heads)]
    for c in reversed(range(tiles)):
        at = slice(c * CHUNK, (c + 1) * CHUNK)
        v1 = vs[at, :]
        for h in range(heads):
            pq = pqs[h, at, :]
            dp = mm(das[h, c], pq, 0, 0)
            dp = dp[:, :width] + dp[:, width:] + mm(v1, sums[h].astype(BF), 1, 1)
            zks[h, at, :] = back(pks[h, at, :], dp)
            sums[h] = sums[h] + mm(pq[:, :width], dds[h, at, :], 0, 0)
    for h in range(heads):
        gq = mm(qs[h], zqs[h], 0, 0)
        gk = mm(ks[...], zks[h], 0, 0)
        gq = gq[:, :width] + gq[:, width:]
        gk = gk[:, :width] + gk[:, width:]
        o_ref[h] = jnp.concatenate(
            [gq[:, :half] - gq[:, half:], gk[:, :half] - gk[:, half:]], axis=1
        )


def student(place, q0, q1, k, v, t0, t1, wq, wk, loss_scale):
    blocks, rows, width = k.shape
    n = blocks * rows
    tiles = n // CHUNK
    whole = pl.BlockSpec(memory_space=pltpu.VMEM)
    wide = pltpu.VMEM((2, n, 2 * width), BF)
    return pl.pallas_call(
        functools.partial(student_kernel, loss_scale),
        out_shape=jax.ShapeDtypeStruct((2, width, width), F32),
        in_specs=[pl.BlockSpec(memory_space=pltpu.SMEM)] + [whole] * 8,
        out_specs=whole,
        scratch_shapes=[
            pltpu.VMEM((2, n, width), BF),
            pltpu.VMEM((n, width), BF),
            pltpu.VMEM((n, 2 * width), BF),
            pltpu.VMEM((2, n, width), BF),
            wide,
            wide,
            wide,
            wide,
            pltpu.VMEM((2, tiles, CHUNK, CHUNK), BF),
            wide,
        ],
        compiler_params=pltpu.CompilerParams(vmem_limit_bytes=56 * 2**20),
        cost_estimate=pl.CostEstimate(
            flops=64 * n * width * CHUNK, bytes_accessed=12 * n * width, transcendentals=4 * n * width
        ),
        name="student",
    )(place, q0, q1, k, v, t0, t1, wq, wk)


def exchange(x, axis):
    return lax.all_to_all(x, axis, split_axis=0, concat_axis=0, tiled=True)


def sum_over(x, axis):
    size = lax.axis_size(axis)
    step = size // 2
    while step:
        x = x + lax.ppermute(x, axis, [(i, i ^ step) for i in range(size)])
        step //= 2
    return x


def on_device(queries, keys, values, block_order, query_maps, key_maps):
    rows = queries.shape[0]
    ctx = lax.axis_size("ctx")
    heads, width, half = query_maps.shape
    kv_heads = keys.shape[1] // width
    shared = ctx // kv_heads
    ids = jnp.arange(ctx, dtype=jnp.int32)
    place = jnp.sum(jnp.where(block_order[0][:, None] == ids[None, :], ids[:, None], 0), axis=0)

    def spread(x):
        x = x.reshape(rows, kv_heads, width).transpose(1, 0, 2)
        return jnp.repeat(x, shared, axis=0)

    by_head = queries.reshape(rows, ctx, heads, width).transpose(2, 1, 0, 3)
    first = exchange(jnp.concatenate([spread(keys), spread(values), by_head[0]], axis=2), "ctx")
    k, v, q0 = jnp.split(first, 3, axis=2)
    q1 = exchange(by_head[1], "ctx")
    t0 = teacher(place, q0, k, v)
    t1 = teacher(place, q1, k, v)
    back = exchange(jnp.concatenate([t0, t1], axis=2), "ctx")
    teacher_out = back.transpose(1, 0, 2).reshape(rows, ctx * heads * width)
    grads = student(place, q0, q1, k, v, t0, t1, query_maps, key_maps, 1.0 / lax.axis_size("dp"))
    grads = sum_over(grads, "dp")
    return teacher_out, grads[:, :, :half], grads[:, :, half:]


def solution(mesh):
    in_specs = (
        P(("dp", "ctx"), None),
        P(("dp", "ctx"), None),
        P(("dp", "ctx"), None),
        P("dp", None),
        P("ctx", None, None),
        P("ctx", None, None),
    )
    out_specs = (P(("dp", "ctx"), None), P("ctx", None, None), P("ctx", None, None))
    return jax.shard_map(
        on_device, mesh=mesh, in_specs=in_specs, out_specs=out_specs, check_vma=False
    )
```

time: 1020 us -> 146 us (0.14)
  the two profiles are of different devices: /device:TPU:2 before, /device:TPU:224 now
where the time goes in v1:
time: 146 us; the launch traced here: 143 us
  Pallas kernels  47.9 us (33%)
  blocking collectives  35.7 us (24%)
  waiting for transfers between devices  27.2 us (19%)
  starting transfers between devices  15.4 us (11%)
  local copies, waits for them, and re-layouts  12.8 us (9%)
  other arithmetic  2.77 us (2%)
    all_to_all x1, blocking collectives, exchange(): return lax.all_to_all(x, axis, split_axis=0, concat_axis=0, tiled=True)  35.7 us
    pallas_call x1, Pallas kernels, student(): pl.pallas_call(functools.partial(student_kernel, loss_scale), out_shape=j...  33.5 us
    ppermute x4, waiting for transfers between devices, sum_over(): x = x + lax.ppermute(x, axis, [(i, i ^ step) for i in range(size)])  23.6 us
    pallas_call x2, Pallas kernels, teacher(): pl.pallas_call(functools.partial(teacher_kernel, math.log2(math.e) * widt...  14.5 us
    ppermute x4, starting transfers between devices, sum_over(): x = x + lax.ppermute(x, axis, [(i, i ^ step) for i in range(size)])  7.8 us
    all_to_all x2, starting transfers between devices, exchange(): return lax.all_to_all(x, axis, split_axis=0, concat_axis=0, tiled=True)  7.63 us
    unnamed x30, local copies, waits for them, and re-layouts  4.76 us
    all_to_all x2, waiting for transfers between devices, exchange(): return lax.all_to_all(x, axis, split_axis=0, concat_axis=0, tiled=True)  3.62 us
  transfers between devices with their start and end apart: 6, of which 5 were waited for; matrix products, arithmetic and copies ran while one was open for 4% of the time, Pallas kernels for 28%

profile of v1, /device:TPU:224, one launch (start us, length us, event | category | flops | bytes accessed | tf_op | source)
XLA Modules:
  0.0 143.0 jit_solution(13784417307562017134)
XLA Ops:
  0.6 2.8 %reshape.29 = bf16[192,16,2,128]{3,2,1,0:T(2,128)(2,1)S(1)} reshape(bf16[192,4096]{1,0:T(8,128)(2,1)} %param.6) | data formatting | bytes 3145728 | tf_op jit(solution)/shard_map/reshape | solution.py:263
  3.5 0.6 copy.33
  4.1 1.0 slice_bitcast_fusion.1
  5.3 0.1 broadcast_in_dim.22
  5.4 0.1 broadcast_in_dim.23
  5.6 0.4 pad_maximum_fusion
  6.0 35.7 %all_to_all.15 = bf16[16,192,384]{2,1,0:T(8,128)(2,1)} all-to-all(bf16[16,192,384]{2,1,0:T(8,128)(2,1)S(1)} %pad_maximum_fusion), channel_id=1, replica_groups=mesh['dp'=16,'ctx'=16] {'ctx'}, dimensions={0} | all-to-all | bytes 4718592 | tf_op jit(solution)/shard_map/all_to_all | solution.py:238
  41.6 3.8 %all-to-all-start.1 = ((bf16[16,192,128]{2,1,0:T(8,128)(2,1)}), bf16[16,192,128]{2,1,0:T(8,128)(2,1)S(1)}, u32[]{:S(2)}, u32[]{:S(2)}) async-start(bf16[16,192,128]{2,1,0:T(8,128)(2,1)} %get-tuple-element.16), calls=%async_computation.1 | async-start | bytes 1572864 | tf_op jit(solution)/shard_map/all_to_all | solution.py:238
  45.5 1.8 %fusion = (bf16[16,192,128]{2,1,0:T(8,128)(2,1)S(1)}, bf16[16,192,128]{2,1,0:T(8,128)(2,1)S(1)}, bf16[16,192,128]{2,1,0:T(8,128)(2,1)S(1)}) fusion(bf16[16,192,384]{2,1,0:T(8,128)(2,1)} %all_to_all.15), kind=kLoop, calls=%fused_computation.7 | loop fusion | bytes 4718592 | tf_op jit(solution)/shard_map/split | solution.py:265
  47.3 7.0 %teacher.2.t0 = bf16[16,192,128]{2,1,0:T(8,128)(2,1)S(1)} custom-call(s32[16]{0:T(128)S(1)} %select_reduce_fusion.place, bf16[16,192,128]{2,1,0:T(8,128)(2,1)S(1)} %get-tuple-element.12.q_ref.q0, bf16[16,192,128]{2,1,0:T(8,128)(2,1)S(1)} %get-tuple-element.14.k_ref, bf16[16,192,128]{2,1,0:T(8,128)(2,1)S(1)} %get-tuple-element.13.v_ref), custom_call_target="tpu_custom_call" | custom-call | flops 2415919104 | bytes 3145728 | tf_op jit(solution)/shard_map/teacher/pallas_call | solution.py:83
  54.4 0.9 copy-done.4
  55.3 3.6 %all-to-all-done.1.q_ref.q1 = bf16[16,192,128]{2,1,0:T(8,128)(2,1)S(1)} async-done(((bf16[16,192,128]{2,1,0:T(8,128)(2,1)}), bf16[16,192,128]{2,1,0:T(8,128)(2,1)S(1)}, u32[]{:S(2)}, u32[]{:S(2)}) %all-to-all-start.1) | async-done | bytes 786464 | tf_op jit(solution)/shard_map/all_to_all | solution.py:238
  58.9 7.5 %teacher.3.t1 = bf16[16,192,128]{2,1,0:T(8,128)(2,1)S(1)} custom-call(s32[16]{0:T(128)S(1)} %select_reduce_fusion.place, bf16[16,192,128]{2,1,0:T(8,128)(2,1)S(1)} %all-to-all-done.1.q_ref.q1, bf16[16,192,128]{2,1,0:T(8,128)(2,1)S(1)} %get-tuple-element.14.k_ref, bf16[16,192,128]{2,1,0:T(8,128)(2,1)S(1)} %get-tuple-element.13.v_ref), custom_call_target="tpu_custom_call" | custom-call | flops 2415919104 | bytes 3145728 | tf_op jit(solution)/shard_map/teacher/pallas_call | solution.py:83
  66.4 0.9 copy-done.6
  67.3 1.4 pad_maximum_fusion.1
  68.6 3.8 %all-to-all-start.2 = ((bf16[16,192,256]{2,1,0:T(8,128)(2,1)}), bf16[16,192,256]{2,1,0:T(8,128)(2,1)S(1)}, u32[]{:S(2)}, u32[]{:S(2)}) async-start(bf16[16,192,256]{2,1,0:T(8,128)(2,1)} %pad_maximum_fusion.1), calls=%async_computation.2 | async-start | bytes 3145728 | tf_op jit(solution)/shard_map/all_to_all | solution.py:238
  72.5 0.7 copy.27.wq
  73.3 0.8 copy.28.wk
  74.0 33.5 %student.1 = f32[2,128,128]{2,1,0:T(8,128)} custom-call(s32[16]{0:T(128)} %copy-done.7, bf16[16,192,128]{2,1,0:T(8,128)(2,1)} %copy-done, bf16[16,192,128]{2,1,0:T(8,128)(2,1)} %copy-done.3, bf16[16,192,128]{2,1,0:T(8,128)(2,1)} %copy-done.2, bf16[16,192,128]{2,1,0:T(8,128)(2,1)} %copy-done.1, bf16[16,192,128]{2,1,0:T(8,128)(2,1)} %copy-done.4, ...), custom_call_target="tpu_custom_call" | custom-call | flops 6442450944 | bytes 4718592 | tf_op jit(solution)/shard_map/student/pallas_call | solution.py:212
  107.5 2.9 %collective-permute-start = (f32[2,128,128]{2,1,0:T(8,128)}, f32[2,128,128]{2,1,0:T(8,128)S(1)}, u32[]{:S(2)}, u32[]{:S(2)}) collective-permute-start(f32[2,128,128]{2,1,0:T(8,128)} %student.1), channel_id=1, source_target_pairs={{0,128},{16,144},{32,160},{48,176},{64,192},{80,208},{96,224},{112... | collective-permute-start | bytes 393224 | tf_op jit(solution)/shard_map/ppermute | solution.py:245
  110.4 4.5 %collective-permute-done = f32[2,128,128]{2,1,0:T(8,128)S(1)} collective-permute-done((f32[2,128,128]{2,1,0:T(8,128)}, f32[2,128,128]{2,1,0:T(8,128)S(1)}, u32[]{:S(2)}, u32[]{:S(2)}) %collective-permute-start) | collective-permute-done | bytes 131104 | tf_op jit(solution)/shard_map/ppermute | solution.py:245
  114.9 0.9 add.12
  115.8 1.5 %collective-permute-start.1 = (f32[2,128,128]{2,1,0:T(8,128)S(1)}, f32[2,128,128]{2,1,0:T(8,128)S(1)}, u32[]{:S(2)}, u32[]{:S(2)}) collective-permute-start(f32[2,128,128]{2,1,0:T(8,128)S(1)} %add.12), channel_id=1, source_target_pairs={{0,64},{16,80},{32,96},{48,112},{64,0},{80,16},{96,32},{112,48},{1... | collective-permute-start | bytes 393224 | tf_op jit(solution)/shard_map/ppermute | solution.py:245
  117.3 8.4 %collective-permute-done.1 = f32[2,128,128]{2,1,0:T(8,128)S(1)} collective-permute-done((f32[2,128,128]{2,1,0:T(8,128)S(1)}, f32[2,128,128]{2,1,0:T(8,128)S(1)}, u32[]{:S(2)}, u32[]{:S(2)}) %collective-permute-start.1) | collective-permute-done | bytes 131104 | tf_op jit(solution)/shard_map/ppermute | solution.py:245
  125.8 3.3 %collective-permute-start.2 = (f32[2,128,128]{2,1,0:T(8,128)S(1)}, f32[2,128,128]{2,1,0:T(8,128)S(1)}, u32[]{:S(2)}, u32[]{:S(2)}) collective-permute-start(f32[2,128,128]{2,1,0:T(8,128)S(1)} %add.13), channel_id=1, source_target_pairs={{0,32},{16,48},{32,0},{48,16},{64,96},{80,112},{96,64},{112,80},{1... | collective-permute-start | bytes 393224 | tf_op jit(solution)/shard_map/ppermute | solution.py:245
  129.1 5.7 %collective-permute-done.2 = f32[2,128,128]{2,1,0:T(8,128)S(1)} collective-permute-done((f32[2,128,128]{2,1,0:T(8,128)S(1)}, f32[2,128,128]{2,1,0:T(8,128)S(1)}, u32[]{:S(2)}, u32[]{:S(2)}) %collective-permute-start.2) | collective-permute-done | bytes 131104 | tf_op jit(solution)/shard_map/ppermute | solution.py:245
  134.8 0.1 collective-permute-start.3
  134.9 5.0 %collective-permute-done.3 = f32[2,128,128]{2,1,0:T(8,128)S(1)} collective-permute-done((f32[2,128,128]{2,1,0:T(8,128)S(1)}, f32[2,128,128]{2,1,0:T(8,128)S(1)}, u32[]{:S(2)}, u32[]{:S(2)}) %collective-permute-start.3) | collective-permute-done | bytes 131104 | tf_op jit(solution)/shard_map/ppermute | solution.py:245
  139.9 0.1 fusion.1
  140.0 0.7 copy.29
  140.7 0.7 copy.30
  141.4 1.3 copy.31
  (33 shorter events, 0.4 us)
Async XLA Ops:
  4.1 1.0 copy-start.8
  4.1 1.1 copy-start.9
  6.0 39.5 %copy-start.12 = (s32[1,16]{1,0:T(1,128)S(1)}, s32[1,16]{1,0:T(1,128)}, u32[]{:S(2)}) copy-start(s32[1,16]{1,0:T(1,128)} %param.9) | copy-start | bytes 196
  41.6 17.3 %all-to-all-start.1 = ((bf16[16,192,128]{2,1,0:T(8,128)(2,1)}), bf16[16,192,128]{2,1,0:T(8,128)(2,1)S(1)}, u32[]{:S(2)}, u32[]{:S(2)}) async-start(bf16[16,192,128]{2,1,0:T(8,128)(2,1)} %get-tuple-element.16), calls=%async_computation.1 | async-start | bytes 1572864 | tf_op jit(solution)/shard_map/all_to_all | solution.py:238
  45.5 13.4 %copy-start.7 = (s32[16]{0:T(128)}, s32[16]{0:T(128)S(1)}, u32[]{:S(2)}) copy-start(s32[16]{0:T(128)S(1)} %select_reduce_fusion.place) | copy-start | bytes 196
  47.3 7.1 %copy-start = (bf16[16,192,128]{2,1,0:T(8,128)(2,1)}, bf16[16,192,128]{2,1,0:T(8,128)(2,1)S(1)}, u32[]{:S(2)}) copy-start(bf16[16,192,128]{2,1,0:T(8,128)(2,1)S(1)} %get-tuple-element.12.q_ref.q0) | copy-start | bytes 2359300
  47.3 11.6 %copy-start.1 = (bf16[16,192,128]{2,1,0:T(8,128)(2,1)}, bf16[16,192,128]{2,1,0:T(8,128)(2,1)S(1)}, u32[]{:S(2)}) copy-start(bf16[16,192,128]{2,1,0:T(8,128)(2,1)S(1)} %get-tuple-element.13.v_ref) | copy-start | bytes 2359300
  47.3 11.6 %copy-start.2 = (bf16[16,192,128]{2,1,0:T(8,128)(2,1)}, bf16[16,192,128]{2,1,0:T(8,128)(2,1)S(1)}, u32[]{:S(2)}) copy-start(bf16[16,192,128]{2,1,0:T(8,128)(2,1)S(1)} %get-tuple-element.14.k_ref) | copy-start | bytes 2359300
  54.4 0.9 copy-start.4
  58.9 7.5 %copy-start.3 = (bf16[16,192,128]{2,1,0:T(8,128)(2,1)}, bf16[16,192,128]{2,1,0:T(8,128)(2,1)S(1)}, u32[]{:S(2)}) copy-start(bf16[16,192,128]{2,1,0:T(8,128)(2,1)S(1)} %all-to-all-done.1.q_ref.q1) | copy-start | bytes 2359300
  58.9 8.4 %copy-start.5 = (bf16[16,192,128]{2,1,0:T(8,128)(2,1)S(1)}, bf16[16,192,128]{2,1,0:T(8,128)(2,1)}, u32[]{:S(2)}) copy-start(bf16[16,192,128]{2,1,0:T(8,128)(2,1)} %copy-done.4) | copy-start | bytes 2359300
  66.4 0.9 copy-start.6
  68.6 3.9 %copy-start.10 = (f32[2,128,64]{1,2,0:T(8,128)S(1)}, f32[2,128,64]{1,2,0:T(8,128)}, u32[]{:S(2)}) copy-start(f32[2,128,64]{1,2,0:T(8,128)} %param.10) | copy-start | bytes 196612
  68.6 4.6 %copy-start.11 = (f32[2,128,64]{1,2,0:T(8,128)S(1)}, f32[2,128,64]{1,2,0:T(8,128)}, u32[]{:S(2)}) copy-start(f32[2,128,64]{1,2,0:T(8,128)} %param.11) | copy-start | bytes 196612
  68.6 72.8 %all-to-all-start.2 = ((bf16[16,192,256]{2,1,0:T(8,128)(2,1)}), bf16[16,192,256]{2,1,0:T(8,128)(2,1)S(1)}, u32[]{:S(2)}, u32[]{:S(2)}) async-start(bf16[16,192,256]{2,1,0:T(8,128)(2,1)} %pad_maximum_fusion.1), calls=%async_computation.2 | async-start | bytes 3145728 | tf_op jit(solution)/shard_map/all_to_all | solution.py:238
  107.5 7.4 %collective-permute-start = (f32[2,128,128]{2,1,0:T(8,128)}, f32[2,128,128]{2,1,0:T(8,128)S(1)}, u32[]{:S(2)}, u32[]{:S(2)}) collective-permute-start(f32[2,128,128]{2,1,0:T(8,128)} %student.1), channel_id=1, source_target_pairs={{0,128},{16,144},{32,160},{48,176},{64,192},{80,208},{96,224},{112... | collective-permute-start | bytes 393224 | tf_op jit(solution)/shard_map/ppermute | solution.py:245
  115.8 9.9 %collective-permute-start.1 = (f32[2,128,128]{2,1,0:T(8,128)S(1)}, f32[2,128,128]{2,1,0:T(8,128)S(1)}, u32[]{:S(2)}, u32[]{:S(2)}) collective-permute-start(f32[2,128,128]{2,1,0:T(8,128)S(1)} %add.12), channel_id=1, source_target_pairs={{0,64},{16,80},{32,96},{48,112},{64,0},{80,16},{96,32},{112,48},{1... | collective-permute-start | bytes 393224 | tf_op jit(solution)/shard_map/ppermute | solution.py:245
  125.8 9.0 %collective-permute-start.2 = (f32[2,128,128]{2,1,0:T(8,128)S(1)}, f32[2,128,128]{2,1,0:T(8,128)S(1)}, u32[]{:S(2)}, u32[]{:S(2)}) collective-permute-start(f32[2,128,128]{2,1,0:T(8,128)S(1)} %add.13), channel_id=1, source_target_pairs={{0,32},{16,48},{32,0},{48,16},{64,96},{80,112},{96,64},{112,80},{1... | collective-permute-start | bytes 393224 | tf_op jit(solution)/shard_map/ppermute | solution.py:245
  134.8 5.1 %collective-permute-start.3 = (f32[2,128,128]{2,1,0:T(8,128)S(1)}, f32[2,128,128]{2,1,0:T(8,128)S(1)}, u32[]{:S(2)}, u32[]{:S(2)}) collective-permute-start(f32[2,128,128]{2,1,0:T(8,128)S(1)} %add.14), channel_id=1, source_target_pairs={{0,16},{16,0},{32,48},{48,32},{64,80},{80,64},{96,112},{112,96},{1... | collective-permute-start | bytes 393224 | tf_op jit(solution)/shard_map/ppermute | solution.py:245

commit v2 on v1

v2 whole, which is shorter than its diff:
```python
import functools
import math

import jax
import jax.numpy as jnp
from jax import lax
from jax.experimental import pallas as pl
from jax.experimental.pallas import tpu as pltpu
from jax.sharding import PartitionSpec as P

BF = jnp.bfloat16
F32 = jnp.float32
CHUNK = 256
STRIDE = 100
LEAD = 1


def mm(a, b, ca=1, cb=0):
    return lax.dot_general(a, b, (((ca,), (cb,)), ((), ())), preferred_element_type=F32)


def split(x):
    high = x.astype(BF)
    return high, (x - high.astype(F32)).astype(BF)


def join(*parts):
    return jnp.concatenate(parts, axis=1)


def lower_mask():
    rows = lax.broadcasted_iota(jnp.int32, (CHUNK, CHUNK), 0)
    cols = lax.broadcasted_iota(jnp.int32, (CHUNK, CHUNK), 1)
    return cols <= rows


def load(place, blocks, sems, parts):
    copies = []
    for a, part in enumerate(parts):
        for p in range(blocks):
            copy = pltpu.make_async_copy(*part(place[p], p), sems.at[a, p])
            copy.start()
            copies.append(copy)
    for copy in copies:
        copy.wait()


def key_value_parts(place, rows, blocks, width, own_ref, other_ref, kvs):
    core = place[blocks]

    def part(ref, side):
        def one(b, p):
            start = pl.multiple_of(p * 2 * rows + side * rows, 32)
            return ref.at[b, :, pl.ds(0, 2 * width)], kvs.at[pl.ds(start, rows), pl.ds(0, 2 * width)]

        return one

    return [part(own_ref, core), part(other_ref, 1 - core)]


def first_query_parts(rows, width, ref, target):
    def part(side):
        return lambda b, p: (
            ref.at[b, :, pl.ds((2 + side) * width, width)],
            target.at[pl.ds((2 * p + side) * rows, rows)],
        )

    return [part(0), part(1)]


def block_part(ref, lane, width, rows, target):
    return lambda b, p: (ref.at[b, :, pl.ds(lane, width)], target.at[pl.ds(p * rows, rows)])


def run(units):
    active = list(units)
    while active:
        active = [u for u in active if next(u, True) is None]


def staggered(units):
    active = []
    for unit in units:
        active = [u for u in active if next(u, True) is None]
        if next(unit, True) is None:
            active.append(unit)
    run(active)


def head_kernel(head, heads, scale, loss_scale, place, own_ref, other_ref, wq_ref, wk_ref, *refs):
    q_ref, gin_ref = (refs[0], refs[2]) if head else (own_ref, None)
    o_ref, g_ref, qs, kvs, ts, scores, probs, pqs, pks, zqs, zks, das, steps, maps, sems, out_sems, map_sems = refs[-17:]
    blocks, rows, _ = own_ref.shape
    n, width = qs.shape
    half = width // 2
    tiles = n // CHUNK
    parts = key_value_parts(place, rows, blocks, width, own_ref, other_ref, kvs)
    if head == 0:
        parts += first_query_parts(rows, width, q_ref, qs)
    else:
        parts.append(block_part(q_ref, 0, width, 2 * rows, qs))
        for h in range(head):
            g_ref[h] = gin_ref[h]
    kvs[:, 2 * width :] = jnp.ones((n, width), BF)
    map_copies = [
        pltpu.make_async_copy(ref.at[head], maps.at[i], map_sems.at[i])
        for i, ref in enumerate((wq_ref, wk_ref))
    ]
    for copy in map_copies:
        copy.start()
    load(place, blocks, sems, parts)
    for copy in map_copies:
        copy.wait()

    mask = lower_mask()
    lanes = lax.broadcasted_iota(jnp.int32, (CHUNK, width), 1)
    left = lanes < half
    square = (2 * width, 2 * width)
    group = jnp.where(
        lax.broadcasted_iota(jnp.int32, square, 0) // half
        == lax.broadcasted_iota(jnp.int32, square, 1) // half,
        1.0,
        0.0,
    ).astype(BF)
    tops = {}
    finished = set()
    active = []

    def first(i, j):
        s = mm(qs[pl.ds(i * CHUNK, CHUNK), :], kvs[pl.ds(j * CHUNK, CHUNK), :width], 1, 1)
        if i == j:
            s = jnp.where(mask, s, -1e30)
        scores[i % 2, j] = s
        top = functools.reduce(
            jnp.maximum, [s[:, g * width : (g + 1) * width] for g in range(CHUNK // width)]
        )
        tops[i] = top if j == 0 else jnp.maximum(tops[i], top)

    def second(i, j, peak):
        p = jnp.exp2((scores[i % 2, j] - peak) * scale)
        probs[i % 2, :, j * CHUNK : (j + 1) * CHUNK] = p.astype(BF)

    def finish(i):
        keys = (i + 1) * CHUNK
        both = mm(probs[i % 2, :, :keys], kvs[:keys, width:])
        ts[pl.ds(i * CHUNK, CHUNK), :] = (both[:, :width] / both[:, width:]).astype(BF)
        finished.add(i)

    def teach():
        for i in range(tiles + 1):
            if i > 0:
                peak = jnp.max(tops[i - 1], axis=1, keepdims=True)
            for j in range(i + 1):
                if i < tiles:
                    first(i, j)
                if i > 0 and j < i:
                    second(i - 1, j, peak)
                if j % STRIDE == STRIDE - 1:
                    yield
            if i > 0:
                finish(i - 1)
            yield

    def tall(w):
        return join(*split(jnp.concatenate([w, -w], axis=0)))

    def halves_sum(xs):
        if len(xs) == 1:
            return [mm(xs[0].astype(BF), group[:width, :width])]
        total = mm(join(*[x.astype(BF) for x in xs]), group)
        return [total[:, :width], total[:, width:]]

    def features(zs):
        tops = []
        for z in zs:
            top = jnp.max(jnp.where(left, z, -jnp.inf), axis=1, keepdims=True)
            other = jnp.max(jnp.where(left, -jnp.inf, z), axis=1, keepdims=True)
            tops.append(jnp.where(left, top, other))
        yield
        es = [jnp.exp(z - top) for z, top in zip(zs, tops)]
        totals = halves_sum(es)
        yield
        return [join(*split(e / total)) for e, total in zip(es, totals)]

    def back(feats, ds):
        ps = [f[:, :width].astype(F32) + f[:, width:].astype(F32) for f in feats]
        xs = [p * d for p, d in zip(ps, ds)]
        totals = halves_sum(xs)
        yield
        return [join(*split(x - p * total)) for x, p, total in zip(xs, ps, totals)]

    wq = tall(maps[0])
    wk = tall(maps[1])
    carry = [jnp.zeros((width, 2 * width), F32) for _ in range(2)]

    def ahead(c):
        at = slice(c * CHUNK, (c + 1) * CHUNK)
        q, k, v1 = qs[at, :], kvs[at, :width], kvs[at, width:]
        zs = [mm(join(q, q), wq, 1, 1), mm(join(k, k), wk, 1, 1)]
        yield
        pq, pk = yield from features(zs)
        pqs[at, :] = pq
        pks[at, :] = pk
        high = pk[:, :width]
        within = mm(pq, join(high, high), 1, 1)
        step = mm(high, v1, 0, 0)
        yield
        within = jnp.where(mask, within, 0.0).astype(BF)
        state = carry[0].astype(BF)
        carry[0] = carry[0] + step
        both = mm(join(within, pq), jnp.concatenate([v1, state, state], axis=0))
        yield
        inverse = 1.0 / both[:, width:]
        out = both[:, :width] * inverse
        while c not in finished:
            yield
        g = (out - ts[at, :].astype(F32)) * (2.0 * loss_scale)
        dd = jnp.sum(g * out, axis=1, keepdims=True) * -inverse
        yield
        dd_high, dd_low = split(dd)
        dd_pair = jnp.where(lanes == 0, dd_high, jnp.where(lanes == 1, dd_low, jnp.zeros_like(dd_low)))
        d = join((g * inverse).astype(BF), dd_pair)
        da = mm(d, v1, 1, 1)
        past = mm(d, state, 1, 1)
        steps[c] = mm(pq[:, :width], d, 0, 0)
        yield
        da = jnp.where(mask, da, 0.0).astype(BF)
        das[c] = da
        dp = mm(da, pk)
        yield
        dp = dp[:, :width] + dp[:, width:] + past
        (zqs[at, :],) = yield from back([pq], [dp])

    def behind(c):
        at = slice(c * CHUNK, (c + 1) * CHUNK)
        dp = mm(das[c], pqs[at, :], 0, 0)
        past = mm(kvs[at, width:], carry[1].astype(BF), 1, 1)
        carry[1] = carry[1] + steps[c]
        yield
        dp = dp[:, :width] + dp[:, width:] + past
        (zks[at, :],) = yield from back([pks[at, :]], [dp])

    def grad(row, x, z):
        g = mm(x, z, 0, 0)
        g = (g[:, :width] + g[:, width:]).T
        g_ref[head, pl.ds(row, half), :] = g[:half] - g[half:]

    lesson = teach()
    spawned = 0
    while len(finished) < tiles or active:
        before = len(finished)
        if len(finished) < tiles:
            next(lesson, None)
        active = [u for u in active if next(u, True) is None]
        while spawned < min(tiles, len(finished) + LEAD):
            unit = ahead(spawned)
            next(unit)
            active.append(unit)
            spawned += 1
    stores = []
    for p in range(blocks):
        store = pltpu.make_async_copy(
            ts.at[pl.ds(p * 2 * rows, 2 * rows)],
            o_ref.at[place[p], :, pl.ds(head * width, width)],
            out_sems.at[p],
        )
        store.start()
        stores.append(store)
    staggered([behind(c) for c in reversed(range(tiles))])
    grad(0, qs[...], zqs[...])
    grad(half, kvs[:, :width], zks[...])
    for store in stores:
        store.wait()


def one_head(head, place, own, other, wq, wk, loss_scale, *rest):
    blocks, rows, width = own.shape[0], own.shape[1], own.shape[2] // 4
    heads, half, _ = wq.shape
    n = 2 * blocks * rows
    tiles = n // CHUNK
    whole = pl.BlockSpec(memory_space=pltpu.VMEM)
    anywhere = pl.BlockSpec(memory_space=pl.ANY)
    hbm = pl.BlockSpec(memory_space=pltpu.HBM)
    specs = [pl.BlockSpec(memory_space=pltpu.SMEM), anywhere, anywhere, hbm, hbm]
    wide = pltpu.VMEM((n, 2 * width), BF)
    return pl.pallas_call(
        functools.partial(head_kernel, head, heads, math.log2(math.e) * width**-0.5, loss_scale),
        out_shape=(
            jax.ShapeDtypeStruct((blocks, 2 * rows, heads * width), BF),
            jax.ShapeDtypeStruct((heads, 2 * half, width), F32),
        ),
        in_specs=specs + [anywhere, hbm, whole][: len(rest)],
        out_specs=(hbm, whole),
        input_output_aliases={6: 0} if rest else {},
        scratch_shapes=[
            pltpu.VMEM((n, width), BF),
            pltpu.VMEM((n, 3 * width), BF),
            pltpu.VMEM((n, width), BF),
            pltpu.VMEM((2, tiles, CHUNK, CHUNK), F32),
            pltpu.VMEM((2, CHUNK, n), BF),
            wide,
            wide,
            wide,
            wide,
            pltpu.VMEM((tiles, CHUNK, CHUNK), BF),
            pltpu.VMEM((tiles, width, 2 * width), F32),
            pltpu.VMEM((2, half, width), F32),
            pltpu.SemaphoreType.DMA((4, blocks)),
            pltpu.SemaphoreType.DMA((blocks,)),
            pltpu.SemaphoreType.DMA((2,)),
        ],
        compiler_params=pltpu.CompilerParams(vmem_limit_bytes=40 * 2**20),
        cost_estimate=pl.CostEstimate(
            flops=2 * n * n * width + 32 * n * width * CHUNK,
            bytes_accessed=8 * n * width,
            transcendentals=n * n // 2 + 2 * n * width,
        ),
        name="one_head",
    )(place, own, other, wq, wk, *rest)


def pack_kernel(q_ref, k_ref, v_ref, x_ref, y_ref, sems):
    ctx, rows, lanes = x_ref.shape
    width = lanes // 4
    shared = ctx * width // k_ref.shape[1]
    copies = []

    def move(source, target):
        copy = pltpu.make_async_copy(source, target, sems.at[len(copies)])
        copy.start()
        copies.append(copy)

    for c in range(ctx):
        mine = pl.ds(c % 2 * rows, rows)
        kv = pl.ds(c // shared * width, width)
        move(k_ref.at[mine, kv], x_ref.at[c, :, pl.ds(0, width)])
        move(v_ref.at[mine, kv], x_ref.at[c, :, pl.ds(width, width)])
        for side in range(2):
            move(
                q_ref.at[pl.ds(side * rows, rows), pl.ds(2 * c * width, width)],
                x_ref.at[c, :, pl.ds((2 + side) * width, width)],
            )
        move(q_ref.at[:, pl.ds((2 * c + 1) * width, width)], y_ref.at[c])
    for copy in copies:
        copy.wait()


def pack(queries, keys, values, ctx, width):
    rows = queries.shape[0]
    whole = pl.BlockSpec(memory_space=pltpu.VMEM)
    hbm = pl.BlockSpec(memory_space=pltpu.HBM)
    return pl.pallas_call(
        pack_kernel,
        out_shape=(
            jax.ShapeDtypeStruct((ctx, rows // 2, 4 * width), BF),
            jax.ShapeDtypeStruct((ctx, rows, width), BF),
        ),
        in_specs=[hbm] * 3,
        out_specs=(whole, whole),
        scratch_shapes=[pltpu.SemaphoreType.DMA((5 * ctx,))],
        compiler_params=pltpu.CompilerParams(vmem_limit_bytes=16 * 2**20),
        name="pack",
    )(queries, keys, values)


def exchange(x, axis):
    return lax.all_to_all(x, axis, split_axis=0, concat_axis=0, tiled=True)


def sum_over(x, axis):
    size = lax.axis_size(axis)
    for step in (4, 2, 1, 8):
        x = x + lax.ppermute(x, axis, [(i, i ^ step) for i in range(size)])
    return x


def on_device(queries, keys, values, block_order, query_maps, key_maps):
    rows = queries.shape[0]
    ctx = lax.axis_size("ctx")
    heads, width, half = query_maps.shape
    ids = jnp.arange(ctx, dtype=jnp.int32)
    place = jnp.sum(jnp.where(block_order[0][:, None] == ids[None, :], ids[:, None], 0), axis=0)
    place = jnp.append(place, lax.axis_index("ctx") % 2)

    first, second = pack(queries, keys, values, ctx, width)
    own = exchange(first, "ctx")
    other = lax.ppermute(own, "ctx", [(i, i ^ 1) for i in range(ctx)])
    q1 = exchange(second, "ctx")
    maps = query_maps.transpose(0, 2, 1), key_maps.transpose(0, 2, 1)
    scale = 1.0 / lax.axis_size("dp")
    t, grads = one_head(0, place, own, other, *maps, scale)
    t, grads = one_head(1, place, own, other, *maps, scale, q1, t, grads)
    t, grads = lax.optimization_barrier((t, grads))
    teacher_out = exchange(t, "ctx").transpose(1, 0, 2).reshape(rows, ctx * heads * width)
    grads = sum_over(grads, "dp").transpose(0, 2, 1)
    return teacher_out, grads[:, :, :half], grads[:, :, half:]


def solution(mesh):
    in_specs = (
        P(("dp", "ctx"), None),
        P(("dp", "ctx"), None),
        P(("dp", "ctx"), None),
        P("dp", None),
        P("ctx", None, None),
        P("ctx", None, None),
    )
    out_specs = (P(("dp", "ctx"), None), P("ctx", None, None), P("ctx", None, None))
    return jax.shard_map(
        on_device, mesh=mesh, in_specs=in_specs, out_specs=out_specs, check_vma=False
    )
```

time: 146 us -> 114 us (0.78)
  the two profiles are of different devices: /device:TPU:224 before, /device:TPU:2 now
where the time goes in v2:
time: 114 us
  Pallas kernels  37 us (32%)
  starting transfers between devices  27.5 us (24%)
  blocking collectives  24.6 us (22%)
  waiting for transfers between devices  18.3 us (16%)
  local copies, waits for them, and re-layouts  5.25 us (5%)
    pallas_call x2, Pallas kernels, one_head(): pl.pallas_call(functools.partial(head_kernel, head, heads, math.log2(math...  34.7 us
    all_to_all x1, blocking collectives, exchange(): return lax.all_to_all(x, axis, split_axis=0, concat_axis=0, tiled=True)  24.6 us
    ppermute x4, waiting for transfers between devices, sum_over(): x = x + lax.ppermute(x, axis, [(i, i ^ step) for i in range(size)])  18.3 us
    ppermute x4, starting transfers between devices, sum_over(): x = x + lax.ppermute(x, axis, [(i, i ^ step) for i in range(size)])  14.9 us
    all_to_all x2, starting transfers between devices, exchange(): return lax.all_to_all(x, axis, split_axis=0, concat_axis=0, tiled=True)  12 us
    unnamed x12, local copies, waits for them, and re-layouts  3.26 us
    pallas_call x1, Pallas kernels, pack(): pl.pallas_call(pack_kernel, out_shape=(jax.ShapeDtypeStruct((ctx, rows //...  2.32 us
  transfers between devices with their start and end apart: 7, of which 4 were waited for; matrix products, arithmetic and copies ran while one was open for 1% of the time, Pallas kernels for 15%

profile of v2, /device:TPU:2, one launch (start us, length us, event | category | flops | bytes accessed | tf_op | source)
XLA Modules:
  0.0 113.6 jit_solution(300008357760486081)
XLA Ops:
  0.6 0.0 copy-start
  0.6 1.4 %copy-done = bf16[192,4096]{1,0:T(8,128)(2,1)S(1)} copy-done((bf16[192,4096]{1,0:T(8,128)(2,1)S(1)}, bf16[192,4096]{1,0:T(8,128)(2,1)}, u32[]{:S(2)}) %copy-start) | copy-done | bytes 1572888
  2.0 0.0 copy-start.1
  2.0 0.9 copy-done.1
  3.0 0.0 copy-start.2
  3.0 0.9 copy-done.2
  3.9 2.3 %pack.1 = (bf16[16,96,512]{2,1,0:T(8,128)(2,1)S(1)}, bf16[16,192,128]{2,1,0:T(8,128)(2,1)}) custom-call(bf16[192,4096]{1,0:T(8,128)(2,1)S(1)} %copy-done, bf16[192,512]{1,0:T(8,128)(2,1)S(1)} %copy-done.1, bf16[192,512]{1,0:T(8,128)(2,1)S(1)} %copy-done.2), custom_call_target="tpu_custom_call" | custom-call | tf_op jit(solution)/shard_map/pack/pallas_call | solution.py:352
  6.2 24.6 %all_to_all.15.own_ref = bf16[16,96,512]{2,1,0:T(8,128)(2,1)S(1)} all-to-all(bf16[16,96,512]{2,1,0:T(8,128)(2,1)S(1)} %get-tuple-element.9), channel_id=1, replica_groups=mesh['dp'=16,'ctx'=16] {'ctx'}, dimensions={0} | all-to-all | bytes 3145728 | tf_op jit(solution)/shard_map/all_to_all | solution.py:367
  30.8 0.0 copy-start.5
  30.8 0.6 collective-permute-start
  31.5 6.2 %all-to-all-start.1 = ((bf16[16,192,128]{2,1,0:T(8,128)(2,1)}), bf16[16,192,128]{2,1,0:T(8,128)(2,1)S(1)}, u32[]{:S(2)}, u32[]{:S(2)}) async-start(bf16[16,192,128]{2,1,0:T(8,128)(2,1)} %get-tuple-element.10), calls=%async_computation.1 | async-start | bytes 1572864 | tf_op jit(solution)/shard_map/all_to_all | solution.py:367
  37.6 0.0 copy-done.5
  37.6 0.1 select_reduce_fusion
  37.7 0.1 pad_add_fusion.place
  37.8 0.0 collective-permute-done.other_ref
  37.8 0.0 copy-done.3
  37.8 0.0 copy-done.4
  37.8 17.4 %one_head.2 = (bf16[16,192,256]{2,1,0:T(8,128)(2,1)}, f32[2,128,128]{2,1,0:T(8,128)S(1)}) custom-call(s32[17]{0:T(128)S(1)} %pad_add_fusion.place, bf16[16,96,512]{2,1,0:T(8,128)(2,1)S(1)} %all_to_all.15.own_ref, bf16[16,96,512]{2,1,0:T(8,128)(2,1)} %collective-permute-done.other_ref, f32[2,64,128]{2,1,0:T(8,128)S(1)} %bitcast.9, f32[2,64,128]{2,1,0:T(8,128)S(1)} %bitcast.11), custom_call_target="tpu_custom_call" | custom-call | flops 5637144576 | bytes 3145728 | tf_op jit(solution)/shard_map/one_head/pallas_call | solution.py:286
  55.2 0.0 all-to-all-done.1.refs_0_
  55.2 17.3 %one_head.3 = (bf16[16,192,256]{2,1,0:T(8,128)(2,1)}, f32[2,128,128]{2,1,0:T(8,128)S(1)}) custom-call(s32[17]{0:T(128)S(1)} %pad_add_fusion.place, bf16[16,96,512]{2,1,0:T(8,128)(2,1)S(1)} %all_to_all.15.own_ref, bf16[16,96,512]{2,1,0:T(8,128)(2,1)} %collective-permute-done.other_ref, f32[2,64,128]{2,1,0:T(8,128)S(1)} %bitcast.10, ...), custom_call_target="tpu_custom_call", output_to_operand_aliasing={{0}: (6, {})} | custom-call | flops 5637144576 | bytes 3145728 | tf_op jit(solution)/shard_map/one_head/pallas_call | solution.py:286
  72.5 5.8 %all-to-all-start.2 = ((bf16[16,192,256]{2,1,0:T(8,128)(2,1)}), bf16[16,192,256]{2,1,0:T(8,128)(2,1)S(1)}, u32[]{:S(2)}, u32[]{:S(2)}) async-start(bf16[16,192,256]{2,1,0:T(8,128)(2,1)} %get-tuple-element.13), calls=%async_computation.2 | async-start | bytes 3145728 | tf_op jit(solution)/shard_map/all_to_all | solution.py:367
  78.3 7.2 %collective-permute-start.1 = (f32[2,128,128]{2,1,0:T(8,128)S(1)}, f32[2,128,128]{2,1,0:T(8,128)S(1)}, u32[]{:S(2)}, u32[]{:S(2)}) collective-permute-start(f32[2,128,128]{2,1,0:T(8,128)S(1)} %get-tuple-element.14), channel_id=1, source_target_pairs={{0,64},{16,80},{32,96},{48,112},{64,0},{80,16},{96,32},{112,48},{1... | collective-permute-start | bytes 393224 | tf_op jit(solution)/shard_map/ppermute | solution.py:373
  85.5 3.9 %collective-permute-done.1 = f32[2,128,128]{2,1,0:T(8,128)S(1)} collective-permute-done((f32[2,128,128]{2,1,0:T(8,128)S(1)}, f32[2,128,128]{2,1,0:T(8,128)S(1)}, u32[]{:S(2)}, u32[]{:S(2)}) %collective-permute-start.1) | collective-permute-done | bytes 131104 | tf_op jit(solution)/shard_map/ppermute | solution.py:373
  89.4 4.7 %collective-permute-start.2 = (f32[2,128,128]{2,1,0:T(8,128)S(1)}, f32[2,128,128]{2,1,0:T(8,128)S(1)}, u32[]{:S(2)}, u32[]{:S(2)}) collective-permute-start(f32[2,128,128]{2,1,0:T(8,128)S(1)} %add.17), channel_id=1, source_target_pairs={{0,32},{16,48},{32,0},{48,16},{64,96},{80,112},{96,64},{112,80},{1... | collective-permute-start | bytes 393224 | tf_op jit(solution)/shard_map/ppermute | solution.py:373
  94.1 5.9 %collective-permute-done.2 = f32[2,128,128]{2,1,0:T(8,128)S(1)} collective-permute-done((f32[2,128,128]{2,1,0:T(8,128)S(1)}, f32[2,128,128]{2,1,0:T(8,128)S(1)}, u32[]{:S(2)}, u32[]{:S(2)}) %collective-permute-start.2) | collective-permute-done | bytes 131104 | tf_op jit(solution)/shard_map/ppermute | solution.py:373
  100.0 0.1 collective-permute-start.3
  100.1 5.0 %collective-permute-done.3 = f32[2,128,128]{2,1,0:T(8,128)S(1)} collective-permute-done((f32[2,128,128]{2,1,0:T(8,128)S(1)}, f32[2,128,128]{2,1,0:T(8,128)S(1)}, u32[]{:S(2)}, u32[]{:S(2)}) %collective-permute-start.3) | collective-permute-done | bytes 131104 | tf_op jit(solution)/shard_map/ppermute | solution.py:373
  105.1 3.0 %collective-permute-start.4 = (f32[2,128,128]{2,1,0:T(8,128)S(1)}, f32[2,128,128]{2,1,0:T(8,128)S(1)}, u32[]{:S(2)}, u32[]{:S(2)}) collective-permute-start(f32[2,128,128]{2,1,0:T(8,128)S(1)} %add.19), channel_id=1, source_target_pairs={{0,128},{16,144},{32,160},{48,176},{64,192},{80,208},{96,224},{112... | collective-permute-start | bytes 393224 | tf_op jit(solution)/shard_map/ppermute | solution.py:373
  108.0 3.6 %collective-permute-done.4 = f32[2,128,128]{2,1,0:T(8,128)S(1)} collective-permute-done((f32[2,128,128]{2,1,0:T(8,128)S(1)}, f32[2,128,128]{2,1,0:T(8,128)S(1)}, u32[]{:S(2)}, u32[]{:S(2)}) %collective-permute-start.4) | collective-permute-done | bytes 131104 | tf_op jit(solution)/shard_map/ppermute | solution.py:373
  111.6 0.7 fusion
  112.3 0.0 all-to-all-done.2
  112.3 1.3 %copy.12 = bf16[16,24,8,256]{3,2,0,1:T(8,128)(2,1)} copy(bf16[16,24,8,256]{3,2,1,0:T(8,128)(2,1)S(1)} %bitcast.13) | data formatting | bytes 3145728 | tf_op jit(solution)/shard_map/reshape | solution.py:394
  (6 shorter events, 0.1 us)
Async XLA Ops:
  0.6 1.4 %copy-start = (bf16[192,4096]{1,0:T(8,128)(2,1)S(1)}, bf16[192,4096]{1,0:T(8,128)(2,1)}, u32[]{:S(2)}) copy-start(bf16[192,4096]{1,0:T(8,128)(2,1)} %q_ref.1) | copy-start | bytes 4718596
  2.0 0.9 copy-start.1
  3.0 0.9 copy-start.2
  30.8 6.8 %copy-start.5 = (s32[1,16]{1,0:T(1,128)S(1)}, s32[1,16]{1,0:T(1,128)}, u32[]{:S(2)}) copy-start(s32[1,16]{1,0:T(1,128)} %param.9) | copy-start | bytes 196
  30.8 7.0 %copy-start.3 = (f32[2,128,64]{1,2,0:T(8,128)S(1)}, f32[2,128,64]{1,2,0:T(8,128)}, u32[]{:S(2)}) copy-start(f32[2,128,64]{1,2,0:T(8,128)} %param.10) | copy-start | bytes 196612
  30.8 7.0 %copy-start.4 = (f32[2,128,64]{1,2,0:T(8,128)S(1)}, f32[2,128,64]{1,2,0:T(8,128)}, u32[]{:S(2)}) copy-start(f32[2,128,64]{1,2,0:T(8,128)} %param.11) | copy-start | bytes 196612
  30.8 7.0 %collective-permute-start = (bf16[16,96,512]{2,1,0:T(8,128)(2,1)S(1)}, bf16[16,96,512]{2,1,0:T(8,128)(2,1)}, u32[]{:S(2)}, u32[]{:S(2)}) collective-permute-start(bf16[16,96,512]{2,1,0:T(8,128)(2,1)S(1)} %all_to_all.15.own_ref), channel_id=1, source_target_pairs={{0,1},{1,0},{2,3},{3,2},{4,5},{5,4},{6,7},{7,6},{8,9},{9,8},{10,11... | collective-permute-start | bytes 4718600 | tf_op jit(solution)/shard_map/ppermute | solution.py:387
  31.5 23.7 %all-to-all-start.1 = ((bf16[16,192,128]{2,1,0:T(8,128)(2,1)}), bf16[16,192,128]{2,1,0:T(8,128)(2,1)S(1)}, u32[]{:S(2)}, u32[]{:S(2)}) async-start(bf16[16,192,128]{2,1,0:T(8,128)(2,1)} %get-tuple-element.10), calls=%async_computation.1 | async-start | bytes 1572864 | tf_op jit(solution)/shard_map/all_to_all | solution.py:367
  72.5 39.8 %all-to-all-start.2 = ((bf16[16,192,256]{2,1,0:T(8,128)(2,1)}), bf16[16,192,256]{2,1,0:T(8,128)(2,1)S(1)}, u32[]{:S(2)}, u32[]{:S(2)}) async-start(bf16[16,192,256]{2,1,0:T(8,128)(2,1)} %get-tuple-element.13), calls=%async_computation.2 | async-start | bytes 3145728 | tf_op jit(solution)/shard_map/all_to_all | solution.py:367
  78.3 11.1 %collective-permute-start.1 = (f32[2,128,128]{2,1,0:T(8,128)S(1)}, f32[2,128,128]{2,1,0:T(8,128)S(1)}, u32[]{:S(2)}, u32[]{:S(2)}) collective-permute-start(f32[2,128,128]{2,1,0:T(8,128)S(1)} %get-tuple-element.14), channel_id=1, source_target_pairs={{0,64},{16,80},{32,96},{48,112},{64,0},{80,16},{96,32},{112,48},{1... | collective-permute-start | bytes 393224 | tf_op jit(solution)/shard_map/ppermute | solution.py:373
  89.4 10.5 %collective-permute-start.2 = (f32[2,128,128]{2,1,0:T(8,128)S(1)}, f32[2,128,128]{2,1,0:T(8,128)S(1)}, u32[]{:S(2)}, u32[]{:S(2)}) collective-permute-start(f32[2,128,128]{2,1,0:T(8,128)S(1)} %add.17), channel_id=1, source_target_pairs={{0,32},{16,48},{32,0},{48,16},{64,96},{80,112},{96,64},{112,80},{1... | collective-permute-start | bytes 393224 | tf_op jit(solution)/shard_map/ppermute | solution.py:373
  100.0 5.1 %collective-permute-start.3 = (f32[2,128,128]{2,1,0:T(8,128)S(1)}, f32[2,128,128]{2,1,0:T(8,128)S(1)}, u32[]{:S(2)}, u32[]{:S(2)}) collective-permute-start(f32[2,128,128]{2,1,0:T(8,128)S(1)} %add.18), channel_id=1, source_target_pairs={{0,16},{16,0},{32,48},{48,32},{64,80},{80,64},{96,112},{112,96},{1... | collective-permute-start | bytes 393224 | tf_op jit(solution)/shard_map/ppermute | solution.py:373
  105.1 6.6 %collective-permute-start.4 = (f32[2,128,128]{2,1,0:T(8,128)S(1)}, f32[2,128,128]{2,1,0:T(8,128)S(1)}, u32[]{:S(2)}, u32[]{:S(2)}) collective-permute-start(f32[2,128,128]{2,1,0:T(8,128)S(1)} %add.19), channel_id=1, source_target_pairs={{0,128},{16,144},{32,160},{48,176},{64,192},{80,208},{96,224},{112... | collective-permute-start | bytes 393224 | tf_op jit(solution)/shard_map/ppermute | solution.py:373

commit v3 on v2

--- a/solution.py
+++ b/solution.py
@@ -34,42 +34,22 @@
     return cols <= rows
 
 
-def load(place, blocks, sems, parts):
-    copies = []
-    for a, part in enumerate(parts):
-        for p in range(blocks):
-            copy = pltpu.make_async_copy(*part(place[p], p), sems.at[a, p])
-            copy.start()
-            copies.append(copy)
-    for copy in copies:
-        copy.wait()
-
-
-def key_value_parts(place, rows, blocks, width, own_ref, other_ref, kvs):
+def in_order(place, own_ref, other_ref, q_ref, kvs, qs):
+    blocks, rows, _ = own_ref.shape
+    width = qs.shape[1]
     core = place[blocks]
-
-    def part(ref, side):
-        def one(b, p):
+    for p in range(blocks):
+        b = place[p]
+        for ref, side in ((own_ref, core), (other_ref, 1 - core)):
             start = pl.multiple_of(p * 2 * rows + side * rows, 32)
-            return ref.at[b, :, pl.ds(0, 2 * width)], kvs.at[pl.ds(start, rows), pl.ds(0, 2 * width)]
-
-        return one
-
-    return [part(own_ref, core), part(other_ref, 1 - core)]
-
-
-def first_query_parts(rows, width, ref, target):
-    def part(side):
-        return lambda b, p: (
-            ref.at[b, :, pl.ds((2 + side) * width, width)],
-            target.at[pl.ds((2 * p + side) * rows, rows)],
-        )
-
-    return [part(0), part(1)]
-
-
-def block_part(ref, lane, width, rows, target):
-    return lambda b, p: (ref.at[b, :, pl.ds(lane, width)], target.at[pl.ds(p * rows, rows)])
+            kvs[pl.ds(start, rows), : 2 * width] = ref[b, :, : 2 * width]
+        if q_ref is None:
+            for side in range(2):
+                qs[pl.ds((2 * p + side) * rows, rows), :] = own_ref[
+                    b, :, (2 + side) * width : (3 + side) * width
+                ]
+        else:
+            qs[pl.ds(p * 2 * rows, 2 * rows), :] = q_ref[b]
 
 
 def run(units):
@@ -88,40 +68,28 @@
 
 
 def head_kernel(head, heads, scale, loss_scale, place, own_ref, other_ref, wq_ref, wk_ref, *refs):
-    q_ref, gin_ref = (refs[0], refs[2]) if head else (own_ref, None)
-    o_ref, g_ref, qs, kvs, ts, scores, probs, pqs, pks, zqs, zks, das, steps, maps, sems, out_sems, map_sems = refs[-17:]
+    q_ref, gin_ref = (refs[0], refs[2]) if head else (None, None)
+    o_ref, g_ref, qs, kvs, ts, scores, probs, pqs, pks, zqs, zks, das, steps, maps, out_sems, map_sems = refs[-16:]
     blocks, rows, _ = own_ref.shape
     n, width = qs.shape
     half = width // 2
     tiles = n // CHUNK
-    parts = key_value_parts(place, rows, blocks, width, own_ref, other_ref, kvs)
-    if head == 0:
-        parts += first_query_parts(rows, width, q_ref, qs)
-    else:
-        parts.append(block_part(q_ref, 0, width, 2 * rows, qs))
-        for h in range(head):
-            g_ref[h] = gin_ref[h]
-    kvs[:, 2 * width :] = jnp.ones((n, width), BF)
+    for h in range(head):
+        g_ref[h] = gin_ref[h]
     map_copies = [
         pltpu.make_async_copy(ref.at[head], maps.at[i], map_sems.at[i])
         for i, ref in enumerate((wq_ref, wk_ref))
     ]
     for copy in map_copies:
         copy.start()
-    load(place, blocks, sems, parts)
+    kvs[:, 2 * width :] = jnp.ones((n, width), BF)
+    in_order(place, own_ref, other_ref, q_ref, kvs, qs)
     for copy in map_copies:
         copy.wait()
 
     mask = lower_mask()
     lanes = lax.broadcasted_iota(jnp.int32, (CHUNK, width), 1)
     left = lanes < half
-    square = (2 * width, 2 * width)
-    group = jnp.where(
-        lax.broadcasted_iota(jnp.int32, square, 0) // half
-        == lax.broadcasted_iota(jnp.int32, square, 1) // half,
-        1.0,
-        0.0,
-    ).astype(BF)
     tops = {}
     finished = set()
     active = []
@@ -164,11 +132,10 @@
     def tall(w):
         return join(*split(jnp.concatenate([w, -w], axis=0)))
 
-    def halves_sum(xs):
-        if len(xs) == 1:
-            return [mm(xs[0].astype(BF), group[:width, :width])]
-        total = mm(join(*[x.astype(BF) for x in xs]), group)
-        return [total[:, :width], total[:, width:]]
+    def halves_sum(x):
+        one = jnp.sum(jnp.where(left, x, 0.0), axis=1, keepdims=True)
+        two = jnp.sum(jnp.where(left, 0.0, x), axis=1, keepdims=True)
+        return jnp.where(left, one, two)
 
     def features(zs):
         tops = []
@@ -178,14 +145,14 @@
             tops.append(jnp.where(left, top, other))
         yield
         es = [jnp.exp(z - top) for z, top in zip(zs, tops)]
-        totals = halves_sum(es)
+        totals = [halves_sum(e) for e in es]
         yield
         return [join(*split(e / total)) for e, total in zip(es, totals)]
 
     def back(feats, ds):
         ps = [f[:, :width].astype(F32) + f[:, width:].astype(F32) for f in feats]
         xs = [p * d for p, d in zip(ps, ds)]
-        totals = halves_sum(xs)
+        totals = [halves_sum(x) for x in xs]
         yield
         return [join(*split(x - p * total)) for x, p, total in zip(xs, ps, totals)]
 
@@ -279,9 +246,8 @@
     n = 2 * blocks * rows
     tiles = n // CHUNK
     whole = pl.BlockSpec(memory_space=pltpu.VMEM)
-    anywhere = pl.BlockSpec(memory_space=pl.ANY)
     hbm = pl.BlockSpec(memory_space=pltpu.HBM)
-    specs = [pl.BlockSpec(memory_space=pltpu.SMEM), anywhere, anywhere, hbm, hbm]
+    specs = [pl.BlockSpec(memory_space=pltpu.SMEM), whole, whole, hbm, hbm]
     wide = pltpu.VMEM((n, 2 * width), BF)
     return pl.pallas_call(
         functools.partial(head_kernel, head, heads, math.log2(math.e) * width**-0.5, loss_scale),
@@ -289,7 +255,7 @@
             jax.ShapeDtypeStruct((blocks, 2 * rows, heads * width), BF),
             jax.ShapeDtypeStruct((heads, 2 * half, width), F32),
         ),
-        in_specs=specs + [anywhere, hbm, whole][: len(rest)],
+        in_specs=specs + [whole, hbm, whole][: len(rest)],
         out_specs=(hbm, whole),
         input_output_aliases={6: 0} if rest else {},
         scratch_shapes=[
@@ -305,7 +271,6 @@
             pltpu.VMEM((tiles, CHUNK, CHUNK), BF),
             pltpu.VMEM((tiles, width, 2 * width), F32),
             pltpu.VMEM((2, half, width), F32),
-            pltpu.SemaphoreType.DMA((4, blocks)),
             pltpu.SemaphoreType.DMA((blocks,)),
             pltpu.SemaphoreType.DMA((2,)),
         ],
@@ -358,7 +323,7 @@
         in_specs=[hbm] * 3,
         out_specs=(whole, whole),
         scratch_shapes=[pltpu.SemaphoreType.DMA((5 * ctx,))],
-        compiler_params=pltpu.CompilerParams(vmem_limit_bytes=16 * 2**20),
+        compiler_params=pltpu.CompilerParams(vmem_limit_bytes=60 * 2**20),
         name="pack",
     )(queries, keys, values)
 
@@ -367,11 +332,9 @@
     return lax.all_to_all(x, axis, split_axis=0, concat_axis=0, tiled=True)
 
 
-def sum_over(x, axis):
+def add_from(x, axis, step):
     size = lax.axis_size(axis)
-    for step in (4, 2, 1, 8):
-        x = x + lax.ppermute(x, axis, [(i, i ^ step) for i in range(size)])
-    return x
+    return x + lax.ppermute(x, axis, [(i, i ^ step) for i in range(size)])
 
 
 def on_device(queries, keys, values, block_order, query_maps, key_maps):
@@ -392,7 +355,9 @@
     t, grads = one_head(1, place, own, other, *maps, scale, q1, t, grads)
     t, grads = lax.optimization_barrier((t, grads))
     teacher_out = exchange(t, "ctx").transpose(1, 0, 2).reshape(rows, ctx * heads * width)
-    grads = sum_over(grads, "dp").transpose(0, 2, 1)
+    for step in (4, 2, 1, 8):
+        grads = add_from(grads, "dp", step)
+    grads = grads.transpose(0, 2, 1)
     return teacher_out, grads[:, :, :half], grads[:, :, half:]
 
 

time: 114 us -> 108 us (0.947)
  local copies, waits for them, and re-layouts: 5.25 us -> 1.99 us
  Pallas kernels: 37 us -> 33.8 us
    pallas_call x2, Pallas kernels: 34.7 us -> 30.1 us  [one_head(): pl.pallas_call(functools.partial(head_kernel, head, heads, math.log2(math...]
    unnamed x12 -> x6, local copies, waits for them, and re-layouts: 3.26 us -> 0.01 us
    pallas_call x1, Pallas kernels: 2.32 us -> 3.79 us  [pack(): pl.pallas_call(pack_kernel, out_shape=(jax.ShapeDtypeStruct((ctx, rows //...]
  transfers between devices with their start and end apart: 7 -> 7, of which waited for: 4 -> 4; matrix products, arithmetic and copies ran while one was open for 1% -> 1% of each run, Pallas kernels for 15% -> 14%
where the time goes in v3:
time: 108 us; the launch traced here: 107 us
  Pallas kernels  33.8 us (31%)
  starting transfers between devices  27.6 us (26%)
  blocking collectives  24.8 us (23%)
  waiting for transfers between devices  18.3 us (17%)
  local copies, waits for them, and re-layouts  1.99 us (2%)
    pallas_call x2, Pallas kernels, one_head(): pl.pallas_call(functools.partial(head_kernel, head, heads, math.log2(math...  30.1 us
    all_to_all x1, blocking collectives, exchange(): return lax.all_to_all(x, axis, split_axis=0, concat_axis=0, tiled=True)  24.8 us
    ppermute x4, waiting for transfers between devices, add_from(): return x + lax.ppermute(x, axis, [(i, i ^ step) for i in range(size)])  18.3 us
    ppermute x4, starting transfers between devices, add_from(): return x + lax.ppermute(x, axis, [(i, i ^ step) for i in range(size)])  14.9 us
    all_to_all x2, starting transfers between devices, exchange(): return lax.all_to_all(x, axis, split_axis=0, concat_axis=0, tiled=True)  12 us
    pallas_call x1, Pallas kernels, pack(): pl.pallas_call(pack_kernel, out_shape=(jax.ShapeDtypeStruct((ctx, rows //...  3.79 us
  transfers between devices with their start and end apart: 7, of which 4 were waited for; matrix products, arithmetic and copies ran while one was open for 1% of the time, Pallas kernels for 14%

profile of v3, /device:TPU:2, one launch (start us, length us, event | category | flops | bytes accessed | tf_op | source)
XLA Modules:
  0.0 107.4 jit_solution(12338687598851790781)
XLA Ops:
  0.6 3.8 %pack.1 = (bf16[16,96,512]{2,1,0:T(8,128)(2,1)}, bf16[16,192,128]{2,1,0:T(8,128)(2,1)}) custom-call(bf16[192,4096]{1,0:T(8,128)(2,1)} %q_ref.1, bf16[192,512]{1,0:T(8,128)(2,1)} %k_ref.1, bf16[192,512]{1,0:T(8,128)(2,1)} %v_ref.1), custom_call_target="tpu_custom_call" | custom-call | tf_op jit(solution)/shard_map/pack/pallas_call | solution.py:317
  4.4 24.8 %all_to_all.15.own_ref = bf16[16,96,512]{2,1,0:T(8,128)(2,1)S(1)} all-to-all(bf16[16,96,512]{2,1,0:T(8,128)(2,1)} %get-tuple-element.9), channel_id=1, replica_groups=mesh['dp'=16,'ctx'=16] {'ctx'}, dimensions={0} | all-to-all | bytes 3145728 | tf_op jit(solution)/shard_map/all_to_all | solution.py:332
  29.2 0.0 copy-start.2
  29.2 0.0 copy-start
  29.2 0.0 copy-start.1
  29.2 0.6 collective-permute-start
  29.9 6.2 %all-to-all-start.1 = ((bf16[16,192,128]{2,1,0:T(8,128)(2,1)}), bf16[16,192,128]{2,1,0:T(8,128)(2,1)S(1)}, u32[]{:S(2)}, u32[]{:S(2)}) async-start(bf16[16,192,128]{2,1,0:T(8,128)(2,1)} %get-tuple-element.10), calls=%async_computation.1 | async-start | bytes 1572864 | tf_op jit(solution)/shard_map/all_to_all | solution.py:332
  36.1 0.0 copy-done.2
  36.1 0.1 select_reduce_fusion
  36.2 0.1 pad_add_fusion.place
  36.2 0.0 collective-permute-done.other_ref
  36.2 0.0 copy-done
  36.2 0.0 copy-done.1
  36.2 15.1 %one_head.2 = (bf16[16,192,256]{2,1,0:T(8,128)(2,1)}, f32[2,128,128]{2,1,0:T(8,128)S(1)}) custom-call(s32[17]{0:T(128)S(1)} %pad_add_fusion.place, bf16[16,96,512]{2,1,0:T(8,128)(2,1)S(1)} %all_to_all.15.own_ref, bf16[16,96,512]{2,1,0:T(8,128)(2,1)} %collective-permute-done.other_ref, f32[2,64,128]{2,1,0:T(8,128)S(1)} %bitcast.9, f32[2,64,128]{2,1,0:T(8,128)S(1)} %bitcast.11), custom_call_target="tpu_custom_call" | custom-call | flops 5637144576 | bytes 3145728 | tf_op jit(solution)/shard_map/one_head/pallas_call | solution.py:252
  51.3 0.0 all-to-all-done.1.refs_0_
  51.3 15.0 %one_head.3 = (bf16[16,192,256]{2,1,0:T(8,128)(2,1)}, f32[2,128,128]{2,1,0:T(8,128)S(1)}) custom-call(s32[17]{0:T(128)S(1)} %pad_add_fusion.place, bf16[16,96,512]{2,1,0:T(8,128)(2,1)S(1)} %all_to_all.15.own_ref, bf16[16,96,512]{2,1,0:T(8,128)(2,1)} %collective-permute-done.other_ref, f32[2,64,128]{2,1,0:T(8,128)S(1)} %bitcast.10, ...), custom_call_target="tpu_custom_call", output_to_operand_aliasing={{0}: (6, {})} | custom-call | flops 5637144576 | bytes 3145728 | tf_op jit(solution)/shard_map/one_head/pallas_call | solution.py:252
  66.3 5.8 %all-to-all-start.2 = ((bf16[16,192,256]{2,1,0:T(8,128)(2,1)}), bf16[16,192,256]{2,1,0:T(8,128)(2,1)S(1)}, u32[]{:S(2)}, u32[]{:S(2)}) async-start(bf16[16,192,256]{2,1,0:T(8,128)(2,1)} %get-tuple-element.13), calls=%async_computation.2 | async-start | bytes 3145728 | tf_op jit(solution)/shard_map/all_to_all | solution.py:332
  72.1 7.2 %collective-permute-start.1 = (f32[2,128,128]{2,1,0:T(8,128)S(1)}, f32[2,128,128]{2,1,0:T(8,128)S(1)}, u32[]{:S(2)}, u32[]{:S(2)}) collective-permute-start(f32[2,128,128]{2,1,0:T(8,128)S(1)} %get-tuple-element.14), channel_id=1, source_target_pairs={{0,64},{16,80},{32,96},{48,112},{64,0},{80,16},{96,32},{112,48},{1... | collective-permute-start | bytes 393224 | tf_op jit(solution)/shard_map/ppermute | solution.py:337
  79.3 3.9 %collective-permute-done.1 = f32[2,128,128]{2,1,0:T(8,128)S(1)} collective-permute-done((f32[2,128,128]{2,1,0:T(8,128)S(1)}, f32[2,128,128]{2,1,0:T(8,128)S(1)}, u32[]{:S(2)}, u32[]{:S(2)}) %collective-permute-start.1) | collective-permute-done | bytes 131104 | tf_op jit(solution)/shard_map/ppermute | solution.py:337
  83.2 4.7 %collective-permute-start.2 = (f32[2,128,128]{2,1,0:T(8,128)S(1)}, f32[2,128,128]{2,1,0:T(8,128)S(1)}, u32[]{:S(2)}, u32[]{:S(2)}) collective-permute-start(f32[2,128,128]{2,1,0:T(8,128)S(1)} %add.17), channel_id=1, source_target_pairs={{0,32},{16,48},{32,0},{48,16},{64,96},{80,112},{96,64},{112,80},{1... | collective-permute-start | bytes 393224 | tf_op jit(solution)/shard_map/ppermute | solution.py:337
  87.9 5.9 %collective-permute-done.2 = f32[2,128,128]{2,1,0:T(8,128)S(1)} collective-permute-done((f32[2,128,128]{2,1,0:T(8,128)S(1)}, f32[2,128,128]{2,1,0:T(8,128)S(1)}, u32[]{:S(2)}, u32[]{:S(2)}) %collective-permute-start.2) | collective-permute-done | bytes 131104 | tf_op jit(solution)/shard_map/ppermute | solution.py:337
  93.8 0.1 collective-permute-start.3
  93.9 5.0 %collective-permute-done.3 = f32[2,128,128]{2,1,0:T(8,128)S(1)} collective-permute-done((f32[2,128,128]{2,1,0:T(8,128)S(1)}, f32[2,128,128]{2,1,0:T(8,128)S(1)}, u32[]{:S(2)}, u32[]{:S(2)}) %collective-permute-start.3) | collective-permute-done | bytes 131104 | tf_op jit(solution)/shard_map/ppermute | solution.py:337
  98.9 3.0 %collective-permute-start.4 = (f32[2,128,128]{2,1,0:T(8,128)S(1)}, f32[2,128,128]{2,1,0:T(8,128)S(1)}, u32[]{:S(2)}, u32[]{:S(2)}) collective-permute-start(f32[2,128,128]{2,1,0:T(8,128)S(1)} %add.19), channel_id=1, source_target_pairs={{0,128},{16,144},{32,160},{48,176},{64,192},{80,208},{96,224},{112... | collective-permute-start | bytes 393224 | tf_op jit(solution)/shard_map/ppermute | solution.py:337
  101.9 3.6 %collective-permute-done.4 = f32[2,128,128]{2,1,0:T(8,128)S(1)} collective-permute-done((f32[2,128,128]{2,1,0:T(8,128)S(1)}, f32[2,128,128]{2,1,0:T(8,128)S(1)}, u32[]{:S(2)}, u32[]{:S(2)}) %collective-permute-start.4) | collective-permute-done | bytes 131104 | tf_op jit(solution)/shard_map/ppermute | solution.py:337
  105.4 0.7 fusion
  106.1 0.0 all-to-all-done.2
  106.1 1.3 %copy.12 = bf16[16,24,8,256]{3,2,0,1:T(8,128)(2,1)} copy(bf16[16,24,8,256]{3,2,1,0:T(8,128)(2,1)S(1)} %bitcast.13) | data formatting | bytes 3145728 | tf_op jit(solution)/shard_map/reshape | solution.py:357
  (4 shorter events, 0.1 us)
Async XLA Ops:
  29.2 6.8 %copy-start.2 = (s32[1,16]{1,0:T(1,128)S(1)}, s32[1,16]{1,0:T(1,128)}, u32[]{:S(2)}) copy-start(s32[1,16]{1,0:T(1,128)} %param.9) | copy-start | bytes 196
  29.2 7.0 %copy-start = (f32[2,128,64]{1,2,0:T(8,128)S(1)}, f32[2,128,64]{1,2,0:T(8,128)}, u32[]{:S(2)}) copy-start(f32[2,128,64]{1,2,0:T(8,128)} %param.10) | copy-start | bytes 196612
  29.2 7.0 %copy-start.1 = (f32[2,128,64]{1,2,0:T(8,128)S(1)}, f32[2,128,64]{1,2,0:T(8,128)}, u32[]{:S(2)}) copy-start(f32[2,128,64]{1,2,0:T(8,128)} %param.11) | copy-start | bytes 196612
  29.2 7.0 %collective-permute-start = (bf16[16,96,512]{2,1,0:T(8,128)(2,1)S(1)}, bf16[16,96,512]{2,1,0:T(8,128)(2,1)}, u32[]{:S(2)}, u32[]{:S(2)}) collective-permute-start(bf16[16,96,512]{2,1,0:T(8,128)(2,1)S(1)} %all_to_all.15.own_ref), channel_id=1, source_target_pairs={{0,1},{1,0},{2,3},{3,2},{4,5},{5,4},{6,7},{7,6},{8,9},{9,8},{10,11... | collective-permute-start | bytes 4718600 | tf_op jit(solution)/shard_map/ppermute | solution.py:350
  29.9 21.4 %all-to-all-start.1 = ((bf16[16,192,128]{2,1,0:T(8,128)(2,1)}), bf16[16,192,128]{2,1,0:T(8,128)(2,1)S(1)}, u32[]{:S(2)}, u32[]{:S(2)}) async-start(bf16[16,192,128]{2,1,0:T(8,128)(2,1)} %get-tuple-element.10), calls=%async_computation.1 | async-start | bytes 1572864 | tf_op jit(solution)/shard_map/all_to_all | solution.py:332
  66.3 39.8 %all-to-all-start.2 = ((bf16[16,192,256]{2,1,0:T(8,128)(2,1)}), bf16[16,192,256]{2,1,0:T(8,128)(2,1)S(1)}, u32[]{:S(2)}, u32[]{:S(2)}) async-start(bf16[16,192,256]{2,1,0:T(8,128)(2,1)} %get-tuple-element.13), calls=%async_computation.2 | async-start | bytes 3145728 | tf_op jit(solution)/shard_map/all_to_all | solution.py:332
  72.1 11.1 %collective-permute-start.1 = (f32[2,128,128]{2,1,0:T(8,128)S(1)}, f32[2,128,128]{2,1,0:T(8,128)S(1)}, u32[]{:S(2)}, u32[]{:S(2)}) collective-permute-start(f32[2,128,128]{2,1,0:T(8,128)S(1)} %get-tuple-element.14), channel_id=1, source_target_pairs={{0,64},{16,80},{32,96},{48,112},{64,0},{80,16},{96,32},{112,48},{1... | collective-permute-start | bytes 393224 | tf_op jit(solution)/shard_map/ppermute | solution.py:337
  83.2 10.5 %collective-permute-start.2 = (f32[2,128,128]{2,1,0:T(8,128)S(1)}, f32[2,128,128]{2,1,0:T(8,128)S(1)}, u32[]{:S(2)}, u32[]{:S(2)}) collective-permute-start(f32[2,128,128]{2,1,0:T(8,128)S(1)} %add.17), channel_id=1, source_target_pairs={{0,32},{16,48},{32,0},{48,16},{64,96},{80,112},{96,64},{112,80},{1... | collective-permute-start | bytes 393224 | tf_op jit(solution)/shard_map/ppermute | solution.py:337
  93.8 5.1 %collective-permute-start.3 = (f32[2,128,128]{2,1,0:T(8,128)S(1)}, f32[2,128,128]{2,1,0:T(8,128)S(1)}, u32[]{:S(2)}, u32[]{:S(2)}) collective-permute-start(f32[2,128,128]{2,1,0:T(8,128)S(1)} %add.18), channel_id=1, source_target_pairs={{0,16},{16,0},{32,48},{48,32},{64,80},{80,64},{96,112},{112,96},{1... | collective-permute-start | bytes 393224 | tf_op jit(solution)/shard_map/ppermute | solution.py:337
  98.9 6.6 %collective-permute-start.4 = (f32[2,128,128]{2,1,0:T(8,128)S(1)}, f32[2,128,128]{2,1,0:T(8,128)S(1)}, u32[]{:S(2)}, u32[]{:S(2)}) collective-permute-start(f32[2,128,128]{2,1,0:T(8,128)S(1)} %add.19), channel_id=1, source_target_pairs={{0,128},{16,144},{32,160},{48,176},{64,192},{80,208},{96,224},{112... | collective-permute-start | bytes 393224 | tf_op jit(solution)/shard_map/ppermute | solution.py:337

commit v4 on v3

--- a/solution.py
+++ b/solution.py
@@ -284,45 +284,56 @@
     )(place, own, other, wq, wk, *rest)
 
 
-def pack_kernel(q_ref, k_ref, v_ref, x_ref, y_ref, sems):
-    ctx, rows, lanes = x_ref.shape
+def pack_kernel(q_ref, k_ref, v_ref, x_ref, y_ref, xs, ys, sems, out_sems):
+    ctx, rows, lanes = xs.shape
     width = lanes // 4
     shared = ctx * width // k_ref.shape[1]
-    copies = []
-
-    def move(source, target):
-        copy = pltpu.make_async_copy(source, target, sems.at[len(copies)])
+    copies = [[] for _ in range(ctx)]
+
+    def move(c, source, target):
+        copy = pltpu.make_async_copy(source, target, sems.at[c, len(copies[c])])
         copy.start()
-        copies.append(copy)
+        copies[c].append(copy)
 
     for c in range(ctx):
         mine = pl.ds(c % 2 * rows, rows)
         kv = pl.ds(c // shared * width, width)
-        move(k_ref.at[mine, kv], x_ref.at[c, :, pl.ds(0, width)])
-        move(v_ref.at[mine, kv], x_ref.at[c, :, pl.ds(width, width)])
+        move(c, k_ref.at[mine, kv], xs.at[c, :, pl.ds(0, width)])
+        move(c, v_ref.at[mine, kv], xs.at[c, :, pl.ds(width, width)])
         for side in range(2):
             move(
+                c,
                 q_ref.at[pl.ds(side * rows, rows), pl.ds(2 * c * width, width)],
-                x_ref.at[c, :, pl.ds((2 + side) * width, width)],
+                xs.at[c, :, pl.ds((2 + side) * width, width)],
             )
-        move(q_ref.at[:, pl.ds((2 * c + 1) * width, width)], y_ref.at[c])
-    for copy in copies:
-        copy.wait()
+        move(c, q_ref.at[:, pl.ds((2 * c + 1) * width, width)], ys.at[c])
+    stores = []
+    for c in range(ctx):
+        for copy in copies[c]:
+            copy.wait()
+        for i, (source, target) in enumerate(((xs, x_ref), (ys, y_ref))):
+            store = pltpu.make_async_copy(source.at[c], target.at[c], out_sems.at[c, i])
+            store.start()
+            stores.append(store)
+    for store in stores:
+        store.wait()
 
 
 def pack(queries, keys, values, ctx, width):
     rows = queries.shape[0]
-    whole = pl.BlockSpec(memory_space=pltpu.VMEM)
     hbm = pl.BlockSpec(memory_space=pltpu.HBM)
+    first, second = (ctx, rows // 2, 4 * width), (ctx, rows, width)
     return pl.pallas_call(
         pack_kernel,
-        out_shape=(
-            jax.ShapeDtypeStruct((ctx, rows // 2, 4 * width), BF),
-            jax.ShapeDtypeStruct((ctx, rows, width), BF),
-        ),
+        out_shape=(jax.ShapeDtypeStruct(first, BF), jax.ShapeDtypeStruct(second, BF)),
         in_specs=[hbm] * 3,
-        out_specs=(whole, whole),
-        scratch_shapes=[pltpu.SemaphoreType.DMA((5 * ctx,))],
+        out_specs=(hbm, hbm),
+        scratch_shapes=[
+            pltpu.VMEM(first, BF),
+            pltpu.VMEM(second, BF),
+            pltpu.SemaphoreType.DMA((ctx, 5)),
+            pltpu.SemaphoreType.DMA((ctx, 2)),
+        ],
         compiler_params=pltpu.CompilerParams(vmem_limit_bytes=60 * 2**20),
         name="pack",
     )(queries, keys, values)

time: 108 us -> 107 us (level)
  no operation moved by 1% of the time
where the time goes in v4:
time: 107 us
  Pallas kernels  33.4 us (31%)
  starting transfers between devices  27.5 us (26%)
  blocking collectives  24.8 us (23%)
  waiting for transfers between devices  18.3 us (17%)
  local copies, waits for them, and re-layouts  1.99 us (2%)
    pallas_call x2, Pallas kernels, one_head(): pl.pallas_call(functools.partial(head_kernel, head, heads, math.log2(math...  30.1 us
    all_to_all x1, blocking collectives, exchange(): return lax.all_to_all(x, axis, split_axis=0, concat_axis=0, tiled=True)  24.8 us
    ppermute x4, waiting for transfers between devices, add_from(): return x + lax.ppermute(x, axis, [(i, i ^ step) for i in range(size)])  18.3 us
    ppermute x4, starting transfers between devices, add_from(): return x + lax.ppermute(x, axis, [(i, i ^ step) for i in range(size)])  14.9 us
    all_to_all x2, starting transfers between devices, exchange(): return lax.all_to_all(x, axis, split_axis=0, concat_axis=0, tiled=True)  12 us
    pallas_call x1, Pallas kernels, pack(): pl.pallas_call(pack_kernel, out_shape=(jax.ShapeDtypeStruct(first, BF), j...  3.33 us
  transfers between devices with their start and end apart: 7, of which 4 were waited for; matrix products, arithmetic and copies ran while one was open for 1% of the time, Pallas kernels for 14%

profile of v4, /device:TPU:2, one launch (start us, length us, event | category | flops | bytes accessed | tf_op | source)
XLA Modules:
  0.0 107.0 jit_solution(4225378190464909198)
XLA Ops:
  0.6 3.3 %pack.1 = (bf16[16,96,512]{2,1,0:T(8,128)(2,1)}, bf16[16,192,128]{2,1,0:T(8,128)(2,1)}) custom-call(bf16[192,4096]{1,0:T(8,128)(2,1)} %q_ref.1, bf16[192,512]{1,0:T(8,128)(2,1)} %k_ref.1, bf16[192,512]{1,0:T(8,128)(2,1)} %v_ref.1), custom_call_target="tpu_custom_call" | custom-call | tf_op jit(solution)/shard_map/pack/pallas_call | solution.py:326
  4.0 24.8 %all_to_all.15.own_ref = bf16[16,96,512]{2,1,0:T(8,128)(2,1)S(1)} all-to-all(bf16[16,96,512]{2,1,0:T(8,128)(2,1)} %get-tuple-element.9), channel_id=1, replica_groups=mesh['dp'=16,'ctx'=16] {'ctx'}, dimensions={0} | all-to-all | bytes 3145728 | tf_op jit(solution)/shard_map/all_to_all | solution.py:343
  28.8 0.0 copy-start.2
  28.8 0.0 copy-start
  28.8 0.0 copy-start.1
  28.8 0.6 collective-permute-start
  29.4 6.2 %all-to-all-start.1 = ((bf16[16,192,128]{2,1,0:T(8,128)(2,1)}), bf16[16,192,128]{2,1,0:T(8,128)(2,1)S(1)}, u32[]{:S(2)}, u32[]{:S(2)}) async-start(bf16[16,192,128]{2,1,0:T(8,128)(2,1)} %get-tuple-element.10), calls=%async_computation.1 | async-start | bytes 1572864 | tf_op jit(solution)/shard_map/all_to_all | solution.py:343
  35.6 0.0 copy-done.2
  35.6 0.1 select_reduce_fusion
  35.7 0.1 pad_add_fusion.place
  35.8 0.0 collective-permute-done.other_ref
  35.8 0.0 copy-done
  35.8 0.0 copy-done.1
  35.8 15.1 %one_head.2 = (bf16[16,192,256]{2,1,0:T(8,128)(2,1)}, f32[2,128,128]{2,1,0:T(8,128)S(1)}) custom-call(s32[17]{0:T(128)S(1)} %pad_add_fusion.place, bf16[16,96,512]{2,1,0:T(8,128)(2,1)S(1)} %all_to_all.15.own_ref, bf16[16,96,512]{2,1,0:T(8,128)(2,1)} %collective-permute-done.other_ref, f32[2,64,128]{2,1,0:T(8,128)S(1)} %bitcast.9, f32[2,64,128]{2,1,0:T(8,128)S(1)} %bitcast.11), custom_call_target="tpu_custom_call" | custom-call | flops 5637144576 | bytes 3145728 | tf_op jit(solution)/shard_map/one_head/pallas_call | solution.py:252
  50.8 0.0 all-to-all-done.1.refs_0_
  50.9 15.0 %one_head.3 = (bf16[16,192,256]{2,1,0:T(8,128)(2,1)}, f32[2,128,128]{2,1,0:T(8,128)S(1)}) custom-call(s32[17]{0:T(128)S(1)} %pad_add_fusion.place, bf16[16,96,512]{2,1,0:T(8,128)(2,1)S(1)} %all_to_all.15.own_ref, bf16[16,96,512]{2,1,0:T(8,128)(2,1)} %collective-permute-done.other_ref, f32[2,64,128]{2,1,0:T(8,128)S(1)} %bitcast.10, ...), custom_call_target="tpu_custom_call", output_to_operand_aliasing={{0}: (6, {})} | custom-call | flops 5637144576 | bytes 3145728 | tf_op jit(solution)/shard_map/one_head/pallas_call | solution.py:252
  65.9 5.8 %all-to-all-start.2 = ((bf16[16,192,256]{2,1,0:T(8,128)(2,1)}), bf16[16,192,256]{2,1,0:T(8,128)(2,1)S(1)}, u32[]{:S(2)}, u32[]{:S(2)}) async-start(bf16[16,192,256]{2,1,0:T(8,128)(2,1)} %get-tuple-element.13), calls=%async_computation.2 | async-start | bytes 3145728 | tf_op jit(solution)/shard_map/all_to_all | solution.py:343
  71.7 7.2 %collective-permute-start.1 = (f32[2,128,128]{2,1,0:T(8,128)S(1)}, f32[2,128,128]{2,1,0:T(8,128)S(1)}, u32[]{:S(2)}, u32[]{:S(2)}) collective-permute-start(f32[2,128,128]{2,1,0:T(8,128)S(1)} %get-tuple-element.14), channel_id=1, source_target_pairs={{0,64},{16,80},{32,96},{48,112},{64,0},{80,16},{96,32},{112,48},{1... | collective-permute-start | bytes 393224 | tf_op jit(solution)/shard_map/ppermute | solution.py:348
  78.9 3.9 %collective-permute-done.1 = f32[2,128,128]{2,1,0:T(8,128)S(1)} collective-permute-done((f32[2,128,128]{2,1,0:T(8,128)S(1)}, f32[2,128,128]{2,1,0:T(8,128)S(1)}, u32[]{:S(2)}, u32[]{:S(2)}) %collective-permute-start.1) | collective-permute-done | bytes 131104 | tf_op jit(solution)/shard_map/ppermute | solution.py:348
  82.8 4.7 %collective-permute-start.2 = (f32[2,128,128]{2,1,0:T(8,128)S(1)}, f32[2,128,128]{2,1,0:T(8,128)S(1)}, u32[]{:S(2)}, u32[]{:S(2)}) collective-permute-start(f32[2,128,128]{2,1,0:T(8,128)S(1)} %add.17), channel_id=1, source_target_pairs={{0,32},{16,48},{32,0},{48,16},{64,96},{80,112},{96,64},{112,80},{1... | collective-permute-start | bytes 393224 | tf_op jit(solution)/shard_map/ppermute | solution.py:348
  87.5 5.9 %collective-permute-done.2 = f32[2,128,128]{2,1,0:T(8,128)S(1)} collective-permute-done((f32[2,128,128]{2,1,0:T(8,128)S(1)}, f32[2,128,128]{2,1,0:T(8,128)S(1)}, u32[]{:S(2)}, u32[]{:S(2)}) %collective-permute-start.2) | collective-permute-done | bytes 131104 | tf_op jit(solution)/shard_map/ppermute | solution.py:348
  93.3 0.1 collective-permute-start.3
  93.4 5.0 %collective-permute-done.3 = f32[2,128,128]{2,1,0:T(8,128)S(1)} collective-permute-done((f32[2,128,128]{2,1,0:T(8,128)S(1)}, f32[2,128,128]{2,1,0:T(8,128)S(1)}, u32[]{:S(2)}, u32[]{:S(2)}) %collective-permute-start.3) | collective-permute-done | bytes 131104 | tf_op jit(solution)/shard_map/ppermute | solution.py:348
  98.4 3.0 %collective-permute-start.4 = (f32[2,128,128]{2,1,0:T(8,128)S(1)}, f32[2,128,128]{2,1,0:T(8,128)S(1)}, u32[]{:S(2)}, u32[]{:S(2)}) collective-permute-start(f32[2,128,128]{2,1,0:T(8,128)S(1)} %add.19), channel_id=1, source_target_pairs={{0,128},{16,144},{32,160},{48,176},{64,192},{80,208},{96,224},{112... | collective-permute-start | bytes 393224 | tf_op jit(solution)/shard_map/ppermute | solution.py:348
  101.4 3.6 %collective-permute-done.4 = f32[2,128,128]{2,1,0:T(8,128)S(1)} collective-permute-done((f32[2,128,128]{2,1,0:T(8,128)S(1)}, f32[2,128,128]{2,1,0:T(8,128)S(1)}, u32[]{:S(2)}, u32[]{:S(2)}) %collective-permute-start.4) | collective-permute-done | bytes 131104 | tf_op jit(solution)/shard_map/ppermute | solution.py:348
  105.0 0.7 fusion
  105.6 0.0 all-to-all-done.2
  105.6 1.3 %copy.12 = bf16[16,24,8,256]{3,2,0,1:T(8,128)(2,1)} copy(bf16[16,24,8,256]{3,2,1,0:T(8,128)(2,1)S(1)} %bitcast.13) | data formatting | bytes 3145728 | tf_op jit(solution)/shard_map/reshape | solution.py:368
  (4 shorter events, 0.1 us)
Async XLA Ops:
  28.8 6.8 %copy-start.2 = (s32[1,16]{1,0:T(1,128)S(1)}, s32[1,16]{1,0:T(1,128)}, u32[]{:S(2)}) copy-start(s32[1,16]{1,0:T(1,128)} %param.9) | copy-start | bytes 196
  28.8 7.0 %copy-start = (f32[2,128,64]{1,2,0:T(8,128)S(1)}, f32[2,128,64]{1,2,0:T(8,128)}, u32[]{:S(2)}) copy-start(f32[2,128,64]{1,2,0:T(8,128)} %param.10) | copy-start | bytes 196612
  28.8 7.0 %copy-start.1 = (f32[2,128,64]{1,2,0:T(8,128)S(1)}, f32[2,128,64]{1,2,0:T(8,128)}, u32[]{:S(2)}) copy-start(f32[2,128,64]{1,2,0:T(8,128)} %param.11) | copy-start | bytes 196612
  28.8 7.0 %collective-permute-start = (bf16[16,96,512]{2,1,0:T(8,128)(2,1)S(1)}, bf16[16,96,512]{2,1,0:T(8,128)(2,1)}, u32[]{:S(2)}, u32[]{:S(2)}) collective-permute-start(bf16[16,96,512]{2,1,0:T(8,128)(2,1)S(1)} %all_to_all.15.own_ref), channel_id=1, source_target_pairs={{0,1},{1,0},{2,3},{3,2},{4,5},{5,4},{6,7},{7,6},{8,9},{9,8},{10,11... | collective-permute-start | bytes 4718600 | tf_op jit(solution)/shard_map/ppermute | solution.py:361
  29.4 21.4 %all-to-all-start.1 = ((bf16[16,192,128]{2,1,0:T(8,128)(2,1)}), bf16[16,192,128]{2,1,0:T(8,128)(2,1)S(1)}, u32[]{:S(2)}, u32[]{:S(2)}) async-start(bf16[16,192,128]{2,1,0:T(8,128)(2,1)} %get-tuple-element.10), calls=%async_computation.1 | async-start | bytes 1572864 | tf_op jit(solution)/shard_map/all_to_all | solution.py:343
  65.9 39.8 %all-to-all-start.2 = ((bf16[16,192,256]{2,1,0:T(8,128)(2,1)}), bf16[16,192,256]{2,1,0:T(8,128)(2,1)S(1)}, u32[]{:S(2)}, u32[]{:S(2)}) async-start(bf16[16,192,256]{2,1,0:T(8,128)(2,1)} %get-tuple-element.13), calls=%async_computation.2 | async-start | bytes 3145728 | tf_op jit(solution)/shard_map/all_to_all | solution.py:343
  71.7 11.1 %collective-permute-start.1 = (f32[2,128,128]{2,1,0:T(8,128)S(1)}, f32[2,128,128]{2,1,0:T(8,128)S(1)}, u32[]{:S(2)}, u32[]{:S(2)}) collective-permute-start(f32[2,128,128]{2,1,0:T(8,128)S(1)} %get-tuple-element.14), channel_id=1, source_target_pairs={{0,64},{16,80},{32,96},{48,112},{64,0},{80,16},{96,32},{112,48},{1... | collective-permute-start | bytes 393224 | tf_op jit(solution)/shard_map/ppermute | solution.py:348
  82.8 10.5 %collective-permute-start.2 = (f32[2,128,128]{2,1,0:T(8,128)S(1)}, f32[2,128,128]{2,1,0:T(8,128)S(1)}, u32[]{:S(2)}, u32[]{:S(2)}) collective-permute-start(f32[2,128,128]{2,1,0:T(8,128)S(1)} %add.17), channel_id=1, source_target_pairs={{0,32},{16,48},{32,0},{48,16},{64,96},{80,112},{96,64},{112,80},{1... | collective-permute-start | bytes 393224 | tf_op jit(solution)/shard_map/ppermute | solution.py:348
  93.3 5.1 %collective-permute-start.3 = (f32[2,128,128]{2,1,0:T(8,128)S(1)}, f32[2,128,128]{2,1,0:T(8,128)S(1)}, u32[]{:S(2)}, u32[]{:S(2)}) collective-permute-start(f32[2,128,128]{2,1,0:T(8,128)S(1)} %add.18), channel_id=1, source_target_pairs={{0,16},{16,0},{32,48},{48,32},{64,80},{80,64},{96,112},{112,96},{1... | collective-permute-start | bytes 393224 | tf_op jit(solution)/shard_map/ppermute | solution.py:348
  98.4 6.6 %collective-permute-start.4 = (f32[2,128,128]{2,1,0:T(8,128)S(1)}, f32[2,128,128]{2,1,0:T(8,128)S(1)}, u32[]{:S(2)}, u32[]{:S(2)}) collective-permute-start(f32[2,128,128]{2,1,0:T(8,128)S(1)} %add.19), channel_id=1, source_target_pairs={{0,128},{16,144},{32,160},{48,176},{64,192},{80,208},{96,224},{112... | collective-permute-start | bytes 393224 | tf_op jit(solution)/shard_map/ppermute | solution.py:348
